TPU v7x, 512 devices: a whole 4x8x8 slice. The times are simulated.
512 devices in a mesh: rep: 32 (over x, y), tp: 16 (over z, core).
Axes of the slice: x: 4, y: 8, z: 8, core: 2. Of those that a mesh axis runs over, the one named last changes fastest.
Arguments:
- hidden: bfloat16 [8192, 53248], P('rep', 'tp'), parts along dimension 0, may hold values from -6 to 6
- codes: bfloat16 [53248, 512], P('tp'), may hold values from -8 to 7, as said below
- scales: float32 [416, 512], P('tp'), may hold values from 0.0003 to 0.003
- sign_bits: int32 [53248], P('tp'), may hold values 0 or 1
Outputs:
- projected: bfloat16 [8192, 512], P(('rep', 'tp')), parts along dimension 0
There are 32 independent parts, one for each index of `rep`. A program takes and returns all parts, laid end to end along the dimension named above; an argument that names none is the same for every part. Nothing has to cross between parts.
Inputs may be any that keep to these rules, and one draw needn't show every extreme that they name: `codes`: whole numbers, the 16 levels of a signed 4-bit code.
All inputs are finite; a program needn't handle non-finite values. No bound on the sum of `sign_bits` on one device may be relied on, other than what follows from the above.
Results may differ from a plain program's by a relative error of at most 0.0064.
Values may be sent and summed in bfloat16 or wider, within the bound.
No kernel may reach another device: no remote copies, remote signals or barrier semaphores. Data moves between devices by JAX's collectives and lax.ppermute only.
A program may use at most 64 MiB of HBM per device.

v0:
```python
import math

import jax
import jax.numpy as jnp
from jax import lax
from jax.sharding import PartitionSpec as P


def partner_2(block, axis, stride):
    count = lax.axis_size(axis)
    route = []
    for low in range(count):
        high = low | 1 << stride
        if high != low and high < count:
            route += [(low, high), (high, low)]
    return lax.ppermute(block, axis, route)


def sylvester(matrix_size):
    indices = jnp.arange(matrix_size, dtype=jnp.int32)
    common = jnp.bitwise_and(indices[:, None], indices[None, :])
    parity = jnp.zeros((matrix_size, matrix_size), jnp.int32)
    for place in range(matrix_size.bit_length() - 1):
        parity = parity + jnp.bitwise_and(jnp.right_shift(common, place), 1)
    return 1.0 - 2.0 * jnp.bitwise_and(parity, 1).astype(jnp.float32)


def per_device(hidden, codes, scales, sign_bits):
    row_count, local_width = hidden.shape
    out_width = codes.shape[1]
    tp_count = lax.axis_size("tp")
    signed = jnp.where(sign_bits[None, :] == 1, hidden, -hidden)
    table = sylvester(256).astype(jnp.bfloat16)
    turned = jnp.dot(signed.reshape(-1, 256), table, preferred_element_type=jnp.float32) * 0.0625
    turned = turned.astype(jnp.bfloat16).reshape(row_count, local_width)
    weight = (
        codes.astype(jnp.float32).reshape(local_width // 128, 128, out_width) * scales[:, None, :]
    )
    weight = weight.reshape(local_width, out_width).astype(jnp.bfloat16)
    device_index = lax.axis_index("tp")
    sections = tp_count.bit_length() - 1
    current = turned.astype(jnp.float32)
    for place in range(sections):
        if place == 0:
            partner = partner_2(turned, "tp", 0).astype(jnp.float32)
        else:
            partner = partner_2(current, "tp", place)
        upper_half = jnp.bitwise_and(jnp.right_shift(device_index, place), 1) == 1
        current = jnp.where(upper_half, partner - current, current + partner)
    rotated = (current / math.sqrt(tp_count)).astype(jnp.bfloat16)
    summed = lax.psum_scatter(
        jnp.dot(rotated, weight, preferred_element_type=jnp.float32),
        "tp",
        scatter_dimension=0,
        tiled=True,
    )
    return summed.astype(jnp.bfloat16)


def solution(mesh):
    return jax.shard_map(
        per_device,
        mesh=mesh,
        in_specs=(P("rep", "tp"), P("tp", None), P("tp", None), P("tp")),
        out_specs=P(("rep", "tp"), None),
        check_vma=False,
    )
```

profile of v0, /device:TPU:6, one launch (start us, length us, event | category | flops | bytes accessed | tf_op | source)
XLA Modules:
  0.0 490.6 jit_solution(4270069261645367814)
XLA Ops:
  6.5 0.7 broadcast_compare_fusion
  7.3 1.6 negate_select_fusion
  8.8 2.1 reshape.12
  10.9 2.0 fusion.1
  13.0 3.5 reshape.13
  16.5 1.9 collective-permute-start
  18.4 0.0 copy-done.1
  18.4 3.7 collective-permute-done
  22.1 2.5 fusion.2
  24.6 0.0 copy-start
  24.6 4.3 collective-permute-start.1
  28.9 74.1 %collective-permute-done.1 = f32[256,3328]{1,0:T(8,128)} collective-permute-done((f32[256,3328]{1,0:T(8,128)S(1)}, f32[256,3328]{1,0:T(8,128)}, u32[]{:S(2)}, u32[]{:S(2)}) %collective-permute-start.1) | collective-permute-done | bytes 3407904 | tf_op jit(solution)/shard_map/ppermute | solution.py:16
  103.0 3.4 add_select_fusion.1
  106.4 6.1 %collective-permute-start.2 = (f32[256,3328]{1,0:T(8,128)S(1)}, f32[256,3328]{1,0:T(8,128)}, u32[]{:S(2)}, u32[]{:S(2)}) collective-permute-start(f32[256,3328]{1,0:T(8,128)S(1)} %add_select_fusion.1), channel_id=1, source_target_pairs={{0,4},{4,0},{1,5},{5,1},{2,6},{6,2},{3,7},{7,3},{8,12},{12,8},{9,1... | collective-permute-start | bytes 10223624 | tf_op jit(solution)/shard_map/ppermute | solution.py:16
  112.5 0.0 copy-start.2
  112.5 146.6 %collective-permute-done.2 = f32[256,3328]{1,0:T(8,128)} collective-permute-done((f32[256,3328]{1,0:T(8,128)S(1)}, f32[256,3328]{1,0:T(8,128)}, u32[]{:S(2)}, u32[]{:S(2)}) %collective-permute-start.2) | collective-permute-done | bytes 3407904 | tf_op jit(solution)/shard_map/ppermute | solution.py:16
  259.1 4.0 add_select_fusion
  263.2 8.4 %collective-permute-start.3 = (f32[256,3328]{1,0:T(8,128)}, f32[256,3328]{1,0:T(8,128)S(1)}, u32[]{:S(2)}, u32[]{:S(2)}) collective-permute-start(f32[256,3328]{1,0:T(8,128)} %add_select_fusion), channel_id=1, source_target_pairs={{0,8},{8,0},{1,9},{9,1},{2,10},{10,2},{3,11},{11,3},{4,12},{12,4},... | collective-permute-start | bytes 10223624 | tf_op jit(solution)/shard_map/ppermute | solution.py:16
  271.6 2.6 fusion
  274.2 144.2 %collective-permute-done.3 = f32[256,3328]{1,0:T(8,128)S(1)} collective-permute-done((f32[256,3328]{1,0:T(8,128)}, f32[256,3328]{1,0:T(8,128)S(1)}, u32[]{:S(2)}, u32[]{:S(2)}) %collective-permute-start.3) | collective-permute-done | bytes 3407904 | tf_op jit(solution)/shard_map/ppermute | solution.py:16
  418.4 4.0 fusion.3
  422.4 0.0 reduce-scatter.2.cloned.1.call-update
  422.4 59.9 %reduce-scatter.2.cloned.1.call-done = f32[16,512]{1,0:T(8,128)} async-done(((f32[256,512]{1,0:T(8,128)}), f32[16,512]{1,0:T(8,128)}) %reduce-scatter.2.cloned.1.call-update) | async-done | bytes 32784 | tf_op jit(solution)/shard_map/reduce_scatter | solution.py:51
  482.3 1.4 convert_element_type.35
  (4 shorter events, 0.0 us)
Async XLA Ops:
  6.5 475.8 %reduce-scatter.2.cloned.1.call-start = ((), (), s32[]{:S(2)}) async-start(), calls=%async_computation.1 | async-start | bytes 557056 | tf_op jit(solution)/shard_map/reduce_scatter | solution.py:51
  16.4 1.9 copy-start.1
  16.5 5.6 %collective-permute-start = (bf16[256,3328]{1,0:T(8,128)(2,1)S(1)}, bf16[256,3328]{1,0:T(8,128)(2,1)}, u32[]{:S(2)}, u32[]{:S(2)}) collective-permute-start(bf16[256,3328]{1,0:T(8,128)(2,1)S(1)} %reshape.13), channel_id=1, source_target_pairs={{0,1},{1,0},{2,3},{3,2},{4,5},{5,4},{6,7},{7,6},{8,9},{9,8},{10,11... | collective-permute-start | bytes 5111816 | tf_op jit(solution)/shard_map/ppermute | solution.py:16
  24.6 4.3 copy-start
  24.6 78.4 %collective-permute-start.1 = (f32[256,3328]{1,0:T(8,128)S(1)}, f32[256,3328]{1,0:T(8,128)}, u32[]{:S(2)}, u32[]{:S(2)}) collective-permute-start(f32[256,3328]{1,0:T(8,128)S(1)} %fusion.2), channel_id=1, source_target_pairs={{0,2},{2,0},{1,3},{3,1},{4,6},{6,4},{5,7},{7,5},{8,10},{10,8},{9,1... | collective-permute-start | bytes 10223624 | tf_op jit(solution)/shard_map/ppermute | solution.py:16
  106.4 152.7 %collective-permute-start.2 = (f32[256,3328]{1,0:T(8,128)S(1)}, f32[256,3328]{1,0:T(8,128)}, u32[]{:S(2)}, u32[]{:S(2)}) collective-permute-start(f32[256,3328]{1,0:T(8,128)S(1)} %add_select_fusion.1), channel_id=1, source_target_pairs={{0,4},{4,0},{1,5},{5,1},{2,6},{6,2},{3,7},{7,3},{8,12},{12,8},{9,1... | collective-permute-start | bytes 10223624 | tf_op jit(solution)/shard_map/ppermute | solution.py:16
  112.5 159.1 %copy-start.2 = (f32[26,512]{1,0:T(8,128)S(1)}, f32[26,512]{1,0:T(8,128)}, u32[]{:S(2)}) copy-start(f32[26,512]{1,0:T(8,128)} %param.6) | copy-start | bytes 159748
  263.2 155.3 %collective-permute-start.3 = (f32[256,3328]{1,0:T(8,128)}, f32[256,3328]{1,0:T(8,128)S(1)}, u32[]{:S(2)}, u32[]{:S(2)}) collective-permute-start(f32[256,3328]{1,0:T(8,128)} %add_select_fusion), channel_id=1, source_target_pairs={{0,8},{8,0},{1,9},{9,1},{2,10},{10,2},{3,11},{11,3},{4,12},{12,4},... | collective-permute-start | bytes 10223624 | tf_op jit(solution)/shard_map/ppermute | solution.py:16
Sparse Core Ops, SparseCore 0:
  422.5 59.7 reduce-scatter.1
where the time goes:
time: 491 us
  waiting for transfers between devices  429 us (87%)
  starting transfers between devices  20.7 us (4%)
  other arithmetic  16.2 us (3%)
  between operations  13.5 us (3%)
  matrix products  5.98 us (1%)
  local copies, waits for them, and re-layouts  5.57 us (1%)
    ppermute x4, waiting for transfers between devices, partner_2(): return lax.ppermute(block, axis, route)  369 us
    reduce_scatter x1, waiting for transfers between devices, per_device(): lax.psum_scatter(jnp.dot(rotated, weight, preferred_element_type=jnp.floa...  59.9 us
    ppermute x4, starting transfers between devices, partner_2(): return lax.ppermute(block, axis, route)  20.7 us
    select_n x3, other arithmetic, per_device(): current = jnp.where(upper_half, partner - current, current + partner)  9.93 us
  transfers between devices with their start and end apart: 5, of which 5 were waited for; matrix products, arithmetic and copies ran while one was open for 1% of the time, Pallas kernels for 0%

commit v1 on v0

v1 whole, which is shorter than its diff:
```python
import functools

import jax
import jax.numpy as jnp
from jax import lax
from jax.experimental import pallas as pl
from jax.experimental.pallas import tpu as pltpu
from jax.sharding import Mesh, PartitionSpec as P

BF16 = jnp.bfloat16
F32 = jnp.float32
TURN = 256
GROUP = 128


def sylvester(matrix_size):
    indices = jnp.arange(matrix_size, dtype=jnp.int32)
    common = jnp.bitwise_and(indices[:, None], indices[None, :])
    parity = jnp.zeros((matrix_size, matrix_size), jnp.int32)
    for place in range(matrix_size.bit_length() - 1):
        parity = parity + jnp.bitwise_and(jnp.right_shift(common, place), 1)
    return 1.0 - 2.0 * jnp.bitwise_and(parity, 1).astype(F32)


def parity_sign(a, b, places):
    common = jnp.bitwise_and(a, b)
    parity = functools.reduce(
        jnp.bitwise_xor, [jnp.right_shift(common, place) for place in range(places)]
    )
    return 1.0 - 2.0 * jnp.bitwise_and(parity, 1).astype(F32)


def turn_kernel(hidden_ref, sign_ref, table_ref, out_ref):
    rows, width = hidden_ref.shape
    half = width // 2
    table = table_ref[...]
    for block in range(width // TURN):
        low = block * TURN
        sign = sign_ref[:, low : low + TURN]
        signed = hidden_ref[:, low : low + TURN] * sign
        turned = jnp.dot(signed, table, preferred_element_type=F32).astype(BF16)
        for piece in range(TURN // 128):
            at = low + piece * 128
            part, inside = at // half, at % half
            value = turned[:, piece * 128 : (piece + 1) * 128]
            for copy in range(2):
                out_ref[2 * part + copy, :, inside : inside + 128] = value


def turn(hidden, sign_bits):
    rows, width = hidden.shape
    sign = (2 * sign_bits - 1).astype(BF16)[None, :]
    table = (sylvester(TURN) * (1.0 / 16.0)).astype(BF16)
    return pl.pallas_call(
        turn_kernel,
        out_shape=jax.ShapeDtypeStruct((4, rows, width // 2), BF16),
        cost_estimate=pl.CostEstimate(
            flops=2 * rows * width * TURN, bytes_accessed=10 * rows * width, transcendentals=0
        ),
        compiler_params=pltpu.CompilerParams(vmem_limit_bytes=40 * 1024 * 1024),
    )(hidden, sign, table)


def weight_share(codes, scales, row_at, row_count, col_at, col_count):
    code = lax.dynamic_slice(codes, (row_at, col_at), (row_count, col_count)).astype(F32)
    first = row_at // GROUP
    last = scales.shape[0] - 1
    spot = lax.broadcasted_iota(jnp.int32, (row_count, 1), 0) + row_at
    scale = None
    for step in range((row_count - 1) // GROUP + 2):
        line = lax.dynamic_slice(scales, (jnp.minimum(first + step, last), col_at), (1, col_count))
        scale = line if scale is None else jnp.where(spot // GROUP >= first + step, line, scale)
    return (code * scale).astype(BF16)


def per_device(hidden, codes, scales, sign_bits):
    row_count, local_width = hidden.shape
    out_width = codes.shape[1]
    x_count, y_count = lax.axis_size("x"), lax.axis_size("y")
    z_count, core_count = lax.axis_size("z"), lax.axis_size("core")
    x, y, z, core = (lax.axis_index(name) for name in ("x", "y", "z", "core"))
    part, side = x // 2, x % 2
    half_width, half_out = local_width // 2, out_width // 2
    share = half_width // y_count

    turned = turn(hidden, sign_bits)
    mine = lax.all_to_all(turned, "x", 0, 0, tiled=True)

    weight = weight_share(
        codes, scales, part * half_width + y * share, share, side * half_out, half_out
    )
    other = lax.ppermute(weight, "core", [(0, 1), (1, 0)])
    paired = jnp.where(core == 0, weight.astype(F32), -weight.astype(F32)) + other.astype(F32)
    paired = (paired * 0.5).astype(BF16)
    chips = lax.all_gather(paired, "z")
    signs = parity_sign(jnp.arange(z_count), z, 3) * 0.5
    mixed = jnp.sum(chips.astype(F32) * signs[:, None, None], axis=0).astype(BF16)
    mixed = lax.all_gather(mixed, "y", tiled=True)

    part_sum = jnp.dot(
        mine.reshape(x_count * row_count, half_width), mixed, preferred_element_type=F32
    )
    out_rows = row_count // (z_count * core_count)
    part_sum = part_sum.reshape(x_count, z_count, core_count, out_rows, half_out)
    first, second = part_sum[:, :, 0], part_sum[:, :, 1]
    keep = jnp.where(core == 0, first, second)
    give = jnp.where(core == 0, second, first).astype(BF16)
    got = lax.ppermute(give, "core", [(0, 1), (1, 0)])
    chip_sum = (keep + got.astype(F32)).astype(BF16)
    chip_sum = chip_sum.reshape(x_count * z_count, out_rows, half_out)
    parts = lax.all_to_all(chip_sum, ("x", "z"), 0, 0, tiled=True)
    parts = parts.reshape(2, 2, z_count, out_rows, half_out).astype(F32)
    total = jnp.sum(parts, axis=(0, 2))
    return jnp.concatenate([total[0], total[1]], axis=-1).astype(BF16)


def solution(mesh):
    devices = mesh.devices.reshape(4, 8, 8, 2)
    grid = Mesh(devices, ("x", "y", "z", "core"))
    rep, tp = ("x", "y"), ("z", "core")
    return jax.shard_map(
        per_device,
        mesh=grid,
        in_specs=(P(rep, tp), P(tp, None), P(tp, None), P(tp)),
        out_specs=P(rep + tp, None),
        check_vma=False,
    )
```

time: 491 us -> 106 us (0.22)
  waiting for transfers between devices: 429 us -> 2.97 us
  blocking collectives: 0 us -> 75.4 us
  between operations: 13.5 us -> 0.08 us
  other arithmetic: 16.2 us -> 4.83 us
  starting transfers between devices: 20.7 us -> 13.4 us
    ppermute x4 -> x2, waiting for transfers between devices: 369 us -> 2.97 us  [the longest x1 1.5 us: per_device(): got = lax.ppermute(give, 'core', [(0, 1), (1, 0)])]
    reduce_scatter x1 -> x0, waiting for transfers between devices: 59.9 us -> none  [per_device(): lax.psum_scatter(jnp.dot(rotated, weight, preferred_element_type=jnp.floa...]
    all_gather x0 -> x2, blocking collectives: none -> 57.6 us  [the longest x1 29.7 us: per_device(): mixed = lax.all_gather(mixed, 'y', tiled=True)]
    all_to_all x0 -> x1, blocking collectives: none -> 17.8 us  [per_device(): parts = lax.all_to_all(chip_sum, ('x', 'z'), 0, 0, tiled=True)]
    ppermute x4 -> x2, starting transfers between devices: 20.7 us -> 3.83 us  [the longest x1 1.92 us: per_device(): got = lax.ppermute(give, 'core', [(0, 1), (1, 0)])]
    select_n x4 -> x0, other arithmetic: 11.5 us -> none  [the longest x3 9.93 us: per_device(): current = jnp.where(upper_half, partner - current, current + partner)]
    all_to_all x0 -> x1, starting transfers between devices: none -> 9.54 us  [per_device(): mine = lax.all_to_all(turned, 'x', 0, 0, tiled=True)]
    reshape x2 -> x0, local copies, waits for them, and re-layouts: 5.56 us -> none  [the longest x1 3.49 us: per_device(): turned = turned.astype(jnp.bfloat16).reshape(row_count, local_width)]
  transfers between devices with their start and end apart: 5 -> 3, of which waited for: 5 -> 2; matrix products, arithmetic and copies ran while one was open for 1% -> 4% of each run, Pallas kernels for 0% -> 0%
where the time goes in v1:
time: 106 us; the launch traced here: 104 us
  blocking collectives  75.4 us (71%)
  starting transfers between devices  13.4 us (13%)
  other arithmetic  4.83 us (5%)
  waiting for transfers between devices  2.97 us (3%)
  local copies, waits for them, and re-layouts  2.36 us (2%)
  Pallas kernels  2.35 us (2%)
  matrix products  2.28 us (2%)
    all_gather x1, blocking collectives, per_device(): mixed = lax.all_gather(mixed, 'y', tiled=True)  29.7 us
    all_gather x1, blocking collectives, per_device(): chips = lax.all_gather(paired, 'z')  27.8 us
    all_to_all x1, blocking collectives, per_device(): parts = lax.all_to_all(chip_sum, ('x', 'z'), 0, 0, tiled=True)  17.8 us
    all_to_all x1, starting transfers between devices, per_device(): mine = lax.all_to_all(turned, 'x', 0, 0, tiled=True)  9.54 us
    pallas_call x1, Pallas kernels, turn(): pl.pallas_call(turn_kernel, out_shape=jax.ShapeDtypeStruct((4, rows, widt...  2.35 us
    dot_general x1, matrix products, per_device(): jnp.dot(mine.reshape(x_count * row_count, half_width), mixed, preferred_e...  2.28 us
  transfers between devices with their start and end apart: 3, of which 2 were waited for; matrix products, arithmetic and copies ran while one was open for 4% of the time, Pallas kernels for 0%

profile of v1, /device:TPU:6, one launch (start us, length us, event | category | flops | bytes accessed | tf_op | source)
XLA Modules:
  0.0 103.6 jit_solution(9593878308363021170)
XLA Ops:
  0.0 0.3 multiply_convert_fusion.table_ref
  0.3 0.7 add_convert_fusion
  1.0 0.0 copy-start
  1.0 1.4 %copy-done = bf16[256,3328]{1,0:T(8,128)(2,1)S(1)} copy-done((bf16[256,3328]{1,0:T(8,128)(2,1)S(1)}, bf16[256,3328]{1,0:T(8,128)(2,1)}, u32[]{:S(2)}) %copy-start) | copy-done | bytes 1703960
  2.5 2.4 %shard_map.46 = bf16[4,256,1664]{2,1,0:T(8,128)(2,1)} custom-call(bf16[256,3328]{1,0:T(8,128)(2,1)S(1)} %copy-done, bf16[1,3328]{1,0:T(2,128)(2,1)S(1)} %broadcast_in_dim.52.sign_ref, bf16[256,256]{1,0:T(8,128)(2,1)S(1)} %multiply_convert_fusion.table_ref), custom_call_target="tpu_custom_call" | custom-call | flops 436207616 | bytes 8519680 | tf_op jit(solution)/shard_map/pallas_call | solution.py:54
  4.8 9.5 %all-to-all-start = ((bf16[4,256,1664]{2,1,0:T(8,128)(2,1)}), bf16[4,256,1664]{2,1,0:T(8,128)(2,1)S(1)}, u32[]{:S(2)}, u32[]{:S(2)}) async-start(bf16[4,256,1664]{2,1,0:T(8,128)(2,1)} %shard_map.46), calls=%async_computation | async-start | bytes 6815744 | tf_op jit(solution)/shard_map/all_to_all | solution.py:87
  14.4 0.9 fusion.10
  15.3 1.7 %multiply_convert_fusion.1 = bf16[208,256]{1,0:T(8,128)(2,1)} fusion(f32[256]{0:T(256)S(1)} %bitcast.48, f32[256]{0:T(256)S(1)} %bitcast.50, f32[256]{0:T(256)S(1)} %bitcast.46, bf16[3328,512]{1,0:T(8,128)(2,1)} %param.5, s32[]{:T(128)S(6)} %select_n.81, s32[]{:T(128)S(6)} %select_n.83, pred[208]{0:T(512)(128)(4,1)S(1)} %get-tuple-element.10, ...), kind=kLoop, calls=%fused_computation.15 | loop fusion | flops 266240 | bytes 216488 | tf_op jit(solution)/shard_map/convert_element_type | solution.py:73
  16.9 1.9 %collective-permute-start = (bf16[208,256]{1,0:T(8,128)(2,1)}, bf16[208,256]{1,0:T(8,128)(2,1)S(1)}, u32[]{:S(2)}, u32[]{:S(2)}) collective-permute-start(bf16[208,256]{1,0:T(8,128)(2,1)} %multiply_convert_fusion.1), channel_id=1, source_target_pairs={{0,1},{1,0},{2,3},{3,2},{4,5},{5,4},{6,7},{7,6},{8,9},{9,8},{10,11... | collective-permute-start | bytes 319496 | tf_op jit(solution)/shard_map/ppermute | solution.py:92
  18.9 1.5 %collective-permute-done = bf16[208,256]{1,0:T(8,128)(2,1)S(1)} collective-permute-done((bf16[208,256]{1,0:T(8,128)(2,1)}, bf16[208,256]{1,0:T(8,128)(2,1)S(1)}, u32[]{:S(2)}, u32[]{:S(2)}) %collective-permute-start) | collective-permute-done | bytes 106528 | tf_op jit(solution)/shard_map/ppermute | solution.py:92
  20.4 1.0 %fusion.9 = bf16[208,256]{1,0:T(8,128)(2,1)S(1)} fusion(bf16[208,256]{1,0:T(8,128)(2,1)S(1)} %collective-permute-done, pred[]{:T(512)S(6)} %eq.4, f32[256]{0:T(256)S(1)} %bitcast.49, f32[256]{0:T(256)S(1)} %bitcast.51, pred[208]{0:T(512)(128)(4,1)S(1)} %get-tuple-element.10, f32[256]{0:T(256)S(1)} %bitcast.47, pred[208]{0:T(512)(128)(4,1)S(1)} %get-tuple-element.11, ...), kind=kLoop, calls=%fused_computation.14 | loop fusion | flops 638976 | bytes 322985 | tf_op jit(solution)/shard_map/convert_element_type | solution.py:94
  21.4 27.8 %all-gather = bf16[1664,256]{1,0:T(8,128)(2,1)S(1)} all-gather(bf16[208,256]{1,0:T(8,128)(2,1)S(1)} %fusion.9), channel_id=2, replica_groups=mesh['x'=4,'y'=8,'z'=8,'core'=2] {'z'}, dimensions={0}, use_global_device_ids=true | all-gather | bytes 958464 | tf_op jit(solution)/shard_map/all_gather | solution.py:95
  49.2 0.2 fusion
  49.5 29.7 %all_gather.11 = bf16[1664,256]{1,0:T(8,128)(2,1)} all-gather(bf16[208,256]{1,0:T(8,128)(2,1)S(1)} %fusion), channel_id=1, replica_groups=mesh['x'=4,'y'=8,'z'=8,'core'=2] {'y'}, dimensions={0}, use_global_device_ids=true | all-gather | bytes 958464 | tf_op jit(solution)/shard_map/all_gather | solution.py:98
  79.2 0.0 all-to-all-done
  79.2 2.3 %fusion.1 = f32[4,8,2,16,256]{4,3,2,1,0:T(8,128)S(1)} fusion(bf16[4,8,2,16,1664]{4,3,2,1,0:T(8,128)(2,1)S(1)} %bitcast.43, bf16[1664,256]{1,0:T(8,128)(2,1)} %all_gather.11), kind=kOutput, calls=%fused_computation.2 | convolution fusion | flops 872415232 | bytes 5308416 | tf_op jit(solution)/shard_map/dot_general | solution.py:100
  81.5 0.1 fusion.6
  81.6 1.9 %collective-permute-start.1 = (bf16[4,8,16,256]{3,2,1,0:T(8,128)(2,1)S(1)}, bf16[4,8,16,256]{3,2,1,0:T(8,128)(2,1)S(1)}, u32[]{:S(2)}, u32[]{:S(2)}) collective-permute-start(bf16[4,8,16,256]{3,2,1,0:T(8,128)(2,1)S(1)} %fusion.6), channel_id=1, source_target_pairs={{0,1},{1,0},{2,3},{3,2},{4,5},{5,4},{6,7},{7,6},{8,9},{9,8},{10,11... | collective-permute-start | bytes 786440 | tf_op jit(solution)/shard_map/ppermute | solution.py:108
  83.5 1.5 %collective-permute-done.1 = bf16[4,8,16,256]{3,2,1,0:T(8,128)(2,1)S(1)} collective-permute-done((bf16[4,8,16,256]{3,2,1,0:T(8,128)(2,1)S(1)}, bf16[4,8,16,256]{3,2,1,0:T(8,128)(2,1)S(1)}, u32[]{:S(2)}, u32[]{:S(2)}) %collective-permute-start.1) | collective-permute-done | bytes 262176 | tf_op jit(solution)/shard_map/ppermute | solution.py:108
  85.0 0.2 fusion.5
  85.2 17.8 %all_to_all.10 = bf16[32,16,256]{2,1,0:T(8,128)(2,1)S(1)} all-to-all(bf16[32,16,256]{2,1,0:T(8,128)(2,1)S(1)} %bitcast.45), channel_id=1, replica_groups=mesh['x'=4,'y'=8,'z'=8,'core'=2] {'x','z'}, dimensions={0} | all-to-all | bytes 524288 | tf_op jit(solution)/shard_map/all_to_all | solution.py:111
  103.0 0.6 pad_maximum_fusion
  (5 shorter events, 0.1 us)
Async XLA Ops:
  1.0 1.5 %copy-start = (bf16[256,3328]{1,0:T(8,128)(2,1)S(1)}, bf16[256,3328]{1,0:T(8,128)(2,1)}, u32[]{:S(2)}) copy-start(bf16[256,3328]{1,0:T(8,128)(2,1)} %hidden_ref.1) | copy-start | bytes 5111812
  4.8 74.4 %all-to-all-start = ((bf16[4,256,1664]{2,1,0:T(8,128)(2,1)}), bf16[4,256,1664]{2,1,0:T(8,128)(2,1)S(1)}, u32[]{:S(2)}, u32[]{:S(2)}) async-start(bf16[4,256,1664]{2,1,0:T(8,128)(2,1)} %shard_map.46), calls=%async_computation | async-start | bytes 6815744 | tf_op jit(solution)/shard_map/all_to_all | solution.py:87
  16.9 3.4 %collective-permute-start = (bf16[208,256]{1,0:T(8,128)(2,1)}, bf16[208,256]{1,0:T(8,128)(2,1)S(1)}, u32[]{:S(2)}, u32[]{:S(2)}) collective-permute-start(bf16[208,256]{1,0:T(8,128)(2,1)} %multiply_convert_fusion.1), channel_id=1, source_target_pairs={{0,1},{1,0},{2,3},{3,2},{4,5},{5,4},{6,7},{7,6},{8,9},{9,8},{10,11... | collective-permute-start | bytes 319496 | tf_op jit(solution)/shard_map/ppermute | solution.py:92
  81.6 3.4 %collective-permute-start.1 = (bf16[4,8,16,256]{3,2,1,0:T(8,128)(2,1)S(1)}, bf16[4,8,16,256]{3,2,1,0:T(8,128)(2,1)S(1)}, u32[]{:S(2)}, u32[]{:S(2)}) collective-permute-start(bf16[4,8,16,256]{3,2,1,0:T(8,128)(2,1)S(1)} %fusion.6), channel_id=1, source_target_pairs={{0,1},{1,0},{2,3},{3,2},{4,5},{5,4},{6,7},{7,6},{8,9},{9,8},{10,11... | collective-permute-start | bytes 786440 | tf_op jit(solution)/shard_map/ppermute | solution.py:108

commit v2 on v1

v2 whole, which is shorter than its diff:
```python
import jax
import jax.numpy as jnp
from jax import lax
from jax.experimental import pallas as pl
from jax.experimental.pallas import tpu as pltpu
from jax.sharding import Mesh, PartitionSpec as P

BF16 = jnp.bfloat16
F32 = jnp.float32
TURN = 256
GROUP = 128
LANES = 128
STEP = 16
PARTS, SIDES = 2, 2


def sylvester(matrix_size):
    indices = jnp.arange(matrix_size, dtype=jnp.int32)
    common = jnp.bitwise_and(indices[:, None], indices[None, :])
    parity = jnp.zeros((matrix_size, matrix_size), jnp.int32)
    for place in range(matrix_size.bit_length() - 1):
        parity = parity + jnp.bitwise_and(jnp.right_shift(common, place), 1)
    return 1.0 - 2.0 * jnp.bitwise_and(parity, 1).astype(F32)


def params(mib):
    return pltpu.CompilerParams(vmem_limit_bytes=mib * 1024 * 1024)


def weight_kernel(rows, padded, codes_ref, scales_ref, out_ref, code_vmem, sem):
    x, y = lax.axis_index("x"), lax.axis_index("y")
    share = (x // SIDES) * lax.axis_size("y") + y
    low = pl.multiple_of((x % SIDES) * (2 * LANES), 2 * LANES)
    copy = pltpu.make_async_copy(
        codes_ref.at[pl.ds(pl.multiple_of(share * rows, STEP), rows), pl.ds(low, 2 * LANES)],
        code_vmem,
        sem,
    )
    copy.start()
    out_ref[2 * rows :] = jnp.zeros((padded - 2 * rows, LANES), BF16)
    copy.wait()
    for step in range(rows // STEP):
        group = (share * (rows // STEP) + step) // (GROUP // STEP)
        scale = scales_ref[pl.ds(group, 1), pl.ds(low, 2 * LANES)]
        value = code_vmem[step * STEP : (step + 1) * STEP].astype(F32) * scale
        value = value.astype(BF16)
        for side in range(2):
            at = side * rows + step * STEP
            out_ref[at : at + STEP] = value[:, side * LANES : (side + 1) * LANES]


def weight_share(codes, scales, rows, padded):
    return pl.pallas_call(
        lambda *refs: weight_kernel(rows, padded, *refs),
        out_shape=jax.ShapeDtypeStruct((padded, LANES), BF16),
        in_specs=[
            pl.BlockSpec(memory_space=pl.ANY),
            pl.BlockSpec(memory_space=pltpu.VMEM),
        ],
        scratch_shapes=[pltpu.VMEM((rows, 2 * LANES), BF16), pltpu.SemaphoreType.DMA],
        cost_estimate=pl.CostEstimate(
            flops=2 * rows * LANES, bytes_accessed=8 * rows * LANES, transcendentals=0
        ),
        compiler_params=params(56),
    )(codes, scales)


def mix_kernel(count, in_ref, out_ref):
    rows = in_ref.shape[0] // count
    for low in range(0, rows, STEP):
        blocks = [
            in_ref[p * rows + low : p * rows + low + STEP].astype(F32) for p in range(count)
        ]
        stride = 1
        while stride < count:
            for p in range(count):
                if not p & stride:
                    a, b = blocks[p], blocks[p + stride]
                    blocks[p], blocks[p + stride] = a + b, a - b
            stride *= 2
        for q in range(count):
            value = (blocks[q] * (count**-0.5)).astype(BF16)
            for y in range(out_ref.shape[0]):
                out_ref[y, q, low : low + STEP] = value


def mix(parts, tp_count, y_count):
    rows = parts.shape[0] // tp_count
    return pl.pallas_call(
        lambda *refs: mix_kernel(tp_count, *refs),
        out_shape=jax.ShapeDtypeStruct((y_count, tp_count, rows, LANES), BF16),
        cost_estimate=pl.CostEstimate(
            flops=8 * parts.size, bytes_accessed=20 * parts.size, transcendentals=0
        ),
        compiler_params=params(24),
    )(parts)


def turn_kernel(hidden_ref, bits_ref, table_ref, same_ref, other_ref):
    rows, width = hidden_ref.shape
    half = width // PARTS
    own = lax.axis_index("x") // SIDES
    table = table_ref[...]
    for keep in range(PARTS):

        @pl.when(own == keep)
        def _(keep=keep):
            for low in range(0, width, TURN):
                hidden = hidden_ref[:, low : low + TURN]
                plus = bits_ref[:, low : low + TURN] == 1
                signed = hidden * jnp.where(plus, 1.0, -1.0).astype(BF16)
                turned = jnp.dot(signed, table, preferred_element_type=F32).astype(BF16)
                for piece in range(0, TURN, LANES):
                    part, inside = divmod(low + piece, half)
                    out_ref = same_ref if part == keep else other_ref
                    out_ref[:, inside : inside + LANES] = turned[:, piece : piece + LANES]


def turn(hidden, sign_bits):
    rows, width = hidden.shape
    table = (sylvester(TURN) * (1.0 / 16.0)).astype(BF16)
    half = jax.ShapeDtypeStruct((rows, width // PARTS), BF16)
    return pl.pallas_call(
        turn_kernel,
        out_shape=(half, half),
        cost_estimate=pl.CostEstimate(
            flops=2 * rows * width * TURN, bytes_accessed=4 * rows * width, transcendentals=0
        ),
        compiler_params=params(24),
    )(hidden, sign_bits.reshape(1, width), table)


def project_kernel(rows, act0, act1, act2, act3, mixed_ref, out_ref, weight_vmem):
    for y in range(mixed_ref.shape[0]):
        for side in range(2):
            weight_vmem[y * rows : (y + 1) * rows, side * LANES : (side + 1) * LANES] = mixed_ref[
                y, side * rows : (side + 1) * rows
            ]
    x = lax.axis_index("x")
    for flip, act_ref in enumerate((act0, act1, act2, act3)):
        value = jnp.dot(act_ref[...], weight_vmem[...], preferred_element_type=F32)
        out_ref[jnp.bitwise_xor(x, flip)] = value.astype(BF16)


def project(acts, mixed, rows):
    count, half = acts[0].shape
    return pl.pallas_call(
        lambda *refs: project_kernel(rows, *refs),
        out_shape=jax.ShapeDtypeStruct((len(acts), count, 2 * LANES), BF16),
        scratch_shapes=[pltpu.VMEM((half, 2 * LANES), BF16)],
        cost_estimate=pl.CostEstimate(
            flops=len(acts) * 4 * count * half * LANES,
            bytes_accessed=len(acts) * 2 * count * half,
            transcendentals=0,
        ),
        compiler_params=params(24),
    )(*acts, mixed)


def per_device(hidden, codes, scales, sign_bits):
    row_count, local_width = hidden.shape
    x_count, y_count = lax.axis_size("x"), lax.axis_size("y")
    tp_count = lax.axis_size("z") * lax.axis_size("core")
    rows = local_width // PARTS // y_count
    padded = -(-2 * rows // (STEP * tp_count)) * STEP * tp_count

    weight = weight_share(codes, scales, rows, padded)
    pieces = weight.reshape(tp_count, padded // tp_count, LANES)
    pieces = lax.all_to_all(pieces, ("z", "core"), 0, 0, tiled=True)

    same, other = turn(hidden, sign_bits)
    pieces, same, other = lax.optimization_barrier((pieces, same, other))
    acts = [same]
    for flip in range(1, x_count):
        route = [(x, x ^ flip) for x in range(x_count)]
        acts.append(lax.ppermute(same if flip < SIDES else other, "x", route))

    mixed = mix(pieces.reshape(padded, LANES), tp_count, y_count)
    mixed = mixed.reshape(y_count * tp_count, padded // tp_count, LANES)
    mixed = lax.all_to_all(mixed, ("y", "z", "core"), 0, 0, tiled=True)

    part_sum = project(acts, mixed.reshape(y_count, padded, LANES), rows)
    out_rows = row_count // tp_count
    parts = lax.all_to_all(
        part_sum.reshape(x_count * tp_count, out_rows, 2 * LANES), ("x", "z", "core"), 0, 0, tiled=True
    )
    parts = parts.reshape(PARTS, SIDES, tp_count, out_rows, 2 * LANES).astype(F32)
    total = jnp.sum(parts, axis=(0, 2))
    return jnp.concatenate([total[side] for side in range(SIDES)], axis=-1).astype(BF16)


def solution(mesh):
    devices = mesh.devices.reshape(4, 8, 8, 2)
    grid = Mesh(devices, ("x", "y", "z", "core"))
    rep, tp = ("x", "y"), ("z", "core")
    return jax.shard_map(
        per_device,
        mesh=grid,
        in_specs=(P(rep, tp), P(tp, None), P(tp, None), P(tp)),
        out_specs=P(rep + tp, None),
        check_vma=False,
    )
```

time: 106 us -> 113 us (1.066)
  blocking collectives: 75.4 us -> 26.8 us
  waiting for transfers between devices: 2.97 us -> 41.5 us
  starting transfers between devices: 13.4 us -> 30.7 us
  other arithmetic: 4.83 us -> 0.95 us
  Pallas kernels: 2.35 us -> 5.46 us
  local copies, waits for them, and re-layouts: 2.36 us -> 5.15 us
  matrix products: 2.28 us -> 0 us
    all_gather x2 -> x0, blocking collectives: 57.6 us -> none  [the longest x1 29.7 us: per_device(): mixed = lax.all_gather(mixed, 'y', tiled=True)]
    ppermute x2 -> x3, waiting for transfers between devices: 2.97 us -> 34.7 us  [per_device(): acts.append(lax.ppermute(same if flip < SIDES else other, 'x', route))]
    all_to_all x1 -> x2, starting transfers between devices: 9.54 us -> 20.9 us  [the longest x1 10.4 us: per_device(): mixed = lax.all_to_all(mixed, ('y', 'z', 'core'), 0, 0, tiled=True)]
    all_to_all x1, blocking collectives: 17.8 us -> 26.8 us  [per_device(): lax.all_to_all(part_sum.reshape(x_count * tp_count, out_rows, 2 * LANES),...]
    all_to_all x1 -> x2, waiting for transfers between devices: 0.01 us -> 6.84 us  [the longest x1 6.84 us: per_device(): pieces = lax.all_to_all(pieces, ('z', 'core'), 0, 0, tiled=True)]
    ppermute x2 -> x3, starting transfers between devices: 3.83 us -> 9.82 us  [per_device(): acts.append(lax.ppermute(same if flip < SIDES else other, 'x', route))]
    unnamed x2 -> x14, local copies, waits for them, and re-layouts: 1.45 us -> 5.13 us
    convert_element_type x5 -> x0, other arithmetic: 3.67 us -> none  [the longest x1 1.69 us: weight_share(): return (code * scale).astype(BF16)]
  transfers between devices with their start and end apart: 3 -> 5, of which waited for: 2 -> 3; matrix products, arithmetic and copies ran while one was open for 4% -> 0% of each run, Pallas kernels for 0% -> 1%
where the time goes in v2:
time: 113 us; the launch traced here: 111 us
  waiting for transfers between devices  41.5 us (37%)
  starting transfers between devices  30.7 us (27%)
  blocking collectives  26.8 us (24%)
  Pallas kernels  5.46 us (5%)
  local copies, waits for them, and re-layouts  5.15 us (5%)
    ppermute x3, waiting for transfers between devices, per_device(): acts.append(lax.ppermute(same if flip < SIDES else other, 'x', route))  34.7 us
    all_to_all x1, blocking collectives, per_device(): lax.all_to_all(part_sum.reshape(x_count * tp_count, out_rows, 2 * LANES),...  26.8 us
    all_to_all x1, starting transfers between devices, per_device(): mixed = lax.all_to_all(mixed, ('y', 'z', 'core'), 0, 0, tiled=True)  10.4 us
    all_to_all x1, starting transfers between devices, per_device(): pieces = lax.all_to_all(pieces, ('z', 'core'), 0, 0, tiled=True)  10.4 us
    ppermute x3, starting transfers between devices, per_device(): acts.append(lax.ppermute(same if flip < SIDES else other, 'x', route))  9.82 us
    all_to_all x1, waiting for transfers between devices, per_device(): pieces = lax.all_to_all(pieces, ('z', 'core'), 0, 0, tiled=True)  6.84 us
    unnamed x14, local copies, waits for them, and re-layouts  5.13 us
    pallas_call x1, Pallas kernels, weight_share(): pl.pallas_call(lambda *refs: weight_kernel(rows, padded, *refs), out_shap...  2.59 us
  transfers between devices with their start and end apart: 5, of which 3 were waited for; matrix products, arithmetic and copies ran while one was open for 0% of the time, Pallas kernels for 1%

profile of v2, /device:TPU:6, one launch (start us, length us, event | category | flops | bytes accessed | tf_op | source)
XLA Modules:
  0.0 110.7 jit_solution(15318675059394232521)
XLA Ops:
  0.0 2.6 %shard_map.46 = bf16[512,128]{1,0:T(8,128)(2,1)} custom-call(bf16[3328,512]{1,0:T(8,128)(2,1)} %refs_0_.1, f32[26,512]{1,0:T(8,128)} %refs_1_.1), custom_call_target="tpu_custom_call" | custom-call | flops 53248 | bytes 212992 | tf_op jit(solution)/shard_map/pallas_call | solution.py:53
  2.6 10.4 %all-to-all-start = ((bf16[16,32,128]{2,1,0:T(8,128)(2,1)}), bf16[16,32,128]{2,1,0:T(8,128)(2,1)S(1)}, u32[]{:S(2)}, u32[]{:S(2)}) async-start(bf16[16,32,128]{2,1,0:T(8,128)(2,1)} %bitcast.14), calls=%async_computation | async-start | bytes 262144 | tf_op jit(solution)/shard_map/all_to_all | solution.py:169
  13.1 0.3 multiply_convert_fusion.table_ref
  13.3 0.0 copy-done
  13.3 0.6 shard_map.47
  14.0 0.9 copy-done.5
  14.9 6.8 %all-to-all-done = bf16[16,32,128]{2,1,0:T(8,128)(2,1)S(1)} async-done(((bf16[16,32,128]{2,1,0:T(8,128)(2,1)}), bf16[16,32,128]{2,1,0:T(8,128)(2,1)S(1)}, u32[]{:S(2)}, u32[]{:S(2)}) %all-to-all-start) | async-done | bytes 131104 | tf_op jit(solution)/shard_map/all_to_all | solution.py:169
  21.8 1.1 shard_map.48
  22.9 10.4 %all-to-all-start.1 = ((bf16[128,32,128]{2,1,0:T(8,128)(2,1)}), bf16[128,32,128]{2,1,0:T(8,128)(2,1)S(1)}, u32[]{:S(2)}, u32[]{:S(2)}) async-start(bf16[128,32,128]{2,1,0:T(8,128)(2,1)} %bitcast.2), calls=%async_computation.1 | async-start | bytes 2097152 | tf_op jit(solution)/shard_map/all_to_all | solution.py:180
  33.3 2.7 %collective-permute-start = (bf16[256,1664]{1,0:T(8,128)(2,1)S(1)}, bf16[256,1664]{1,0:T(8,128)(2,1)S(1)}, u32[]{:S(2)}, u32[]{:S(2)}) collective-permute-start(bf16[256,1664]{1,0:T(8,128)(2,1)S(1)} %get-tuple-element.12.refs_0_), channel_id=1, source_target_pairs={{0,128},{128,0},{256,384},{384,256},{1,129},{129,1},{257,385},{385... | collective-permute-start | bytes 2555912 | tf_op jit(solution)/shard_map/ppermute | solution.py:176
  36.1 3.0 %collective-permute-start.2 = (bf16[256,1664]{1,0:T(8,128)(2,1)}, bf16[256,1664]{1,0:T(8,128)(2,1)S(1)}, u32[]{:S(2)}, u32[]{:S(2)}) collective-permute-start(bf16[256,1664]{1,0:T(8,128)(2,1)} %copy-done.5), channel_id=1, source_target_pairs={{0,384},{128,256},{256,128},{384,0},{1,385},{129,257},{257,129},{3... | collective-permute-start | bytes 2555912 | tf_op jit(solution)/shard_map/ppermute | solution.py:176
  39.1 4.0 %collective-permute-start.1 = (bf16[256,1664]{1,0:T(8,128)(2,1)}, bf16[256,1664]{1,0:T(8,128)(2,1)S(1)}, u32[]{:S(2)}, u32[]{:S(2)}) collective-permute-start(bf16[256,1664]{1,0:T(8,128)(2,1)} %copy-done.5), channel_id=1, source_target_pairs={{0,256},{128,384},{256,0},{384,128},{1,257},{129,385},{257,1},{385... | collective-permute-start | bytes 2555912 | tf_op jit(solution)/shard_map/ppermute | solution.py:176
  43.2 13.9 %collective-permute-done.refs_1_ = bf16[256,1664]{1,0:T(8,128)(2,1)S(1)} collective-permute-done((bf16[256,1664]{1,0:T(8,128)(2,1)S(1)}, bf16[256,1664]{1,0:T(8,128)(2,1)S(1)}, u32[]{:S(2)}, u32[]{:S(2)}) %collective-permute-start) | collective-permute-done | bytes 852000 | tf_op jit(solution)/shard_map/ppermute | solution.py:176
  57.1 20.7 %collective-permute-done.2.refs_3_ = bf16[256,1664]{1,0:T(8,128)(2,1)S(1)} collective-permute-done((bf16[256,1664]{1,0:T(8,128)(2,1)}, bf16[256,1664]{1,0:T(8,128)(2,1)S(1)}, u32[]{:S(2)}, u32[]{:S(2)}) %collective-permute-start.2) | collective-permute-done | bytes 852000 | tf_op jit(solution)/shard_map/ppermute | solution.py:176
  77.8 0.9 copy-done.1
  78.7 0.0 collective-permute-done.1.refs_2_
  78.7 1.0 copy-done.3
  79.7 0.0 all-to-all-done.1
  79.7 1.2 %copy-done.2 = bf16[256,1664]{1,0:T(8,128)(2,1)S(1)} copy-done((bf16[256,1664]{1,0:T(8,128)(2,1)S(1)}, bf16[256,1664]{1,0:T(8,128)(2,1)}, u32[]{:S(2)}) %copy-start.2) | copy-done | bytes 851992
  80.9 1.2 %copy-done.4 = bf16[256,1664]{1,0:T(8,128)(2,1)S(1)} copy-done((bf16[256,1664]{1,0:T(8,128)(2,1)S(1)}, bf16[256,1664]{1,0:T(8,128)(2,1)}, u32[]{:S(2)}) %copy-start.4) | copy-done | bytes 851992
  82.0 1.1 %shard_map.49 = bf16[4,256,256]{2,1,0:T(8,128)(2,1)S(1)} custom-call(bf16[256,1664]{1,0:T(8,128)(2,1)S(1)} %get-tuple-element.12.refs_0_, bf16[256,1664]{1,0:T(8,128)(2,1)S(1)} %collective-permute-done.refs_1_, bf16[256,1664]{1,0:T(8,128)(2,1)S(1)} %copy-done.4, bf16[256,1664]{1,0:T(8,128)(2,1)S(1)} %copy-done.2, bf16[8,512,128]{2,1,0:T(8,128)(2,1)S(1)} %bitcast.10), custom_call_target="tpu_custom_call" | custom-call | flops 872415232 | bytes 3407872 | tf_op jit(solution)/shard_map/pallas_call | solution.py:147
  83.2 26.8 %all_to_all.15 = bf16[64,16,256]{2,1,0:T(8,128)(2,1)S(1)} all-to-all(bf16[64,16,256]{2,1,0:T(8,128)(2,1)S(1)} %bitcast.11), channel_id=1, replica_groups=mesh['x'=4,'y'=8,'z'=8,'core'=2] {'x','z','core'}, dimensions={0} | all-to-all | bytes 1048576 | tf_op jit(solution)/shard_map/all_to_all | solution.py:184
  109.9 0.1 reduce
  110.0 0.6 pad_maximum_fusion
  (10 shorter events, 0.0 us)
Async XLA Ops:
  0.0 13.0 %copy-start.6 = (s32[3328]{0:T(1024)S(1)}, s32[3328]{0:T(1024)}, u32[]{:S(2)}) copy-start(s32[3328]{0:T(1024)} %param.7) | copy-start | bytes 39940
  0.0 13.3 %copy-start = (bf16[256,3328]{1,0:T(8,128)(2,1)S(1)}, bf16[256,3328]{1,0:T(8,128)(2,1)}, u32[]{:S(2)}) copy-start(bf16[256,3328]{1,0:T(8,128)(2,1)} %hidden_ref.1) | copy-start | bytes 5111812
  2.6 19.2 %all-to-all-start = ((bf16[16,32,128]{2,1,0:T(8,128)(2,1)}), bf16[16,32,128]{2,1,0:T(8,128)(2,1)S(1)}, u32[]{:S(2)}, u32[]{:S(2)}) async-start(bf16[16,32,128]{2,1,0:T(8,128)(2,1)} %bitcast.14), calls=%async_computation | async-start | bytes 262144 | tf_op jit(solution)/shard_map/all_to_all | solution.py:169
  14.0 1.0 copy-start.5
  22.9 56.8 %all-to-all-start.1 = ((bf16[128,32,128]{2,1,0:T(8,128)(2,1)}), bf16[128,32,128]{2,1,0:T(8,128)(2,1)S(1)}, u32[]{:S(2)}, u32[]{:S(2)}) async-start(bf16[128,32,128]{2,1,0:T(8,128)(2,1)} %bitcast.2), calls=%async_computation.1 | async-start | bytes 2097152 | tf_op jit(solution)/shard_map/all_to_all | solution.py:180
  33.3 23.8 %collective-permute-start = (bf16[256,1664]{1,0:T(8,128)(2,1)S(1)}, bf16[256,1664]{1,0:T(8,128)(2,1)S(1)}, u32[]{:S(2)}, u32[]{:S(2)}) collective-permute-start(bf16[256,1664]{1,0:T(8,128)(2,1)S(1)} %get-tuple-element.12.refs_0_), channel_id=1, source_target_pairs={{0,128},{128,0},{256,384},{384,256},{1,129},{129,1},{257,385},{385... | collective-permute-start | bytes 2555912 | tf_op jit(solution)/shard_map/ppermute | solution.py:176
  36.1 41.8 %collective-permute-start.2 = (bf16[256,1664]{1,0:T(8,128)(2,1)}, bf16[256,1664]{1,0:T(8,128)(2,1)S(1)}, u32[]{:S(2)}, u32[]{:S(2)}) collective-permute-start(bf16[256,1664]{1,0:T(8,128)(2,1)} %copy-done.5), channel_id=1, source_target_pairs={{0,384},{128,256},{256,128},{384,0},{1,385},{129,257},{257,129},{3... | collective-permute-start | bytes 2555912 | tf_op jit(solution)/shard_map/ppermute | solution.py:176
  39.1 39.6 %collective-permute-start.1 = (bf16[256,1664]{1,0:T(8,128)(2,1)}, bf16[256,1664]{1,0:T(8,128)(2,1)S(1)}, u32[]{:S(2)}, u32[]{:S(2)}) collective-permute-start(bf16[256,1664]{1,0:T(8,128)(2,1)} %copy-done.5), channel_id=1, source_target_pairs={{0,256},{128,384},{256,0},{384,128},{1,257},{129,385},{257,1},{385... | collective-permute-start | bytes 2555912 | tf_op jit(solution)/shard_map/ppermute | solution.py:176
  77.8 0.9 copy-start.1
  78.7 1.0 copy-start.3
  79.7 1.2 %copy-start.2 = (bf16[256,1664]{1,0:T(8,128)(2,1)S(1)}, bf16[256,1664]{1,0:T(8,128)(2,1)}, u32[]{:S(2)}) copy-start(bf16[256,1664]{1,0:T(8,128)(2,1)} %copy-done.1) | copy-start | bytes 2555908
  80.9 1.2 %copy-start.4 = (bf16[256,1664]{1,0:T(8,128)(2,1)S(1)}, bf16[256,1664]{1,0:T(8,128)(2,1)}, u32[]{:S(2)}) copy-start(bf16[256,1664]{1,0:T(8,128)(2,1)} %copy-done.3) | copy-start | bytes 2555908

commit v3 on v2

--- a/solution.py
+++ b/solution.py
@@ -169,17 +169,17 @@
     pieces = lax.all_to_all(pieces, ("z", "core"), 0, 0, tiled=True)
 
     same, other = turn(hidden, sign_bits)
-    pieces, same, other = lax.optimization_barrier((pieces, same, other))
+    pieces = lax.optimization_barrier((pieces, same, other))[0]
     acts = [same]
     for flip in range(1, x_count):
         route = [(x, x ^ flip) for x in range(x_count)]
         acts.append(lax.ppermute(same if flip < SIDES else other, "x", route))
 
-    mixed = mix(pieces.reshape(padded, LANES), tp_count, y_count)
-    mixed = mixed.reshape(y_count * tp_count, padded // tp_count, LANES)
-    mixed = lax.all_to_all(mixed, ("y", "z", "core"), 0, 0, tiled=True)
-
-    part_sum = project(acts, mixed.reshape(y_count, padded, LANES), rows)
+    mixed = mix(pieces.reshape(padded, LANES), tp_count, 1)
+    mixed = lax.all_to_all(mixed[0], ("z", "core"), 0, 0, tiled=True)
+    mixed = lax.all_gather(mixed.reshape(padded, LANES)[: 2 * rows], "y")
+
+    part_sum = project(acts, mixed, rows)
     out_rows = row_count // tp_count
     parts = lax.all_to_all(
         part_sum.reshape(x_count * tp_count, out_rows, 2 * LANES), ("x", "z", "core"), 0, 0, tiled=True

time: 113 us -> 95.6 us (0.85)
  waiting for transfers between devices: 41.5 us -> 0.01 us
  blocking collectives: 26.8 us -> 66.5 us
  starting transfers between devices: 30.7 us -> 20.8 us
  local copies, waits for them, and re-layouts: 5.15 us -> 0.03 us
    ppermute x3, waiting for transfers between devices: 34.7 us -> 0.01 us  [per_device(): acts.append(lax.ppermute(same if flip < SIDES else other, 'x', route))]
    all_gather x0 -> x1, blocking collectives: none -> 28.1 us  [per_device(): mixed = lax.all_gather(mixed.reshape(padded, LANES)[:2 * rows], 'y')]
    all_to_all x0 -> x1, blocking collectives: none -> 15.8 us  [per_device(): mixed = lax.all_to_all(mixed[0], ('z', 'core'), 0, 0, tiled=True)]
    all_to_all x1 -> x0, starting transfers between devices: 10.4 us -> none  [per_device(): mixed = lax.all_to_all(mixed, ('y', 'z', 'core'), 0, 0, tiled=True)]
    all_to_all x1, waiting for transfers between devices: 6.84 us -> 0.01 us  [per_device(): pieces = lax.all_to_all(pieces, ('z', 'core'), 0, 0, tiled=True)]
    unnamed x14 -> x4, local copies, waits for them, and re-layouts: 5.13 us -> 0.01 us
    all_to_all x1, blocking collectives: 26.8 us -> 22.7 us  [per_device(): lax.all_to_all(part_sum.reshape(x_count * tp_count, out_rows, 2 * LANES),...]
  transfers between devices with their start and end apart: 5 -> 4, of which waited for: 3 -> 0; matrix products, arithmetic and copies ran while one was open for 0% -> 0% of each run, Pallas kernels for 1% -> 2%
where the time goes in v3:
time: 95.6 us; the launch traced here: 93.8 us
  blocking collectives  66.5 us (70%)
  starting transfers between devices  20.8 us (22%)
  Pallas kernels  5.36 us (6%)
    all_gather x1, blocking collectives, per_device(): mixed = lax.all_gather(mixed.reshape(padded, LANES)[:2 * rows], 'y')  28.1 us
    all_to_all x1, blocking collectives, per_device(): lax.all_to_all(part_sum.reshape(x_count * tp_count, out_rows, 2 * LANES),...  22.7 us
    all_to_all x1, blocking collectives, per_device(): mixed = lax.all_to_all(mixed[0], ('z', 'core'), 0, 0, tiled=True)  15.8 us
    all_to_all x1, starting transfers between devices, per_device(): pieces = lax.all_to_all(pieces, ('z', 'core'), 0, 0, tiled=True)  10.4 us
    ppermute x3, starting transfers between devices, per_device(): acts.append(lax.ppermute(same if flip < SIDES else other, 'x', route))  10.4 us
    pallas_call x1, Pallas kernels, weight_share(): pl.pallas_call(lambda *refs: weight_kernel(rows, padded, *refs), out_shap...  2.6 us
  transfers between devices with their start and end apart: 4, of which 0 were waited for; matrix products, arithmetic and copies ran while one was open for 0% of the time, Pallas kernels for 2%

profile of v3, /device:TPU:6, one launch (start us, length us, event | category | flops | bytes accessed | tf_op | source)
XLA Modules:
  0.0 93.8 jit_solution(16073237685747902529)
XLA Ops:
  0.0 0.0 copy-start.1
  0.0 0.0 copy-start
  0.0 2.6 %shard_map.47 = bf16[512,128]{1,0:T(8,128)(2,1)} custom-call(bf16[3328,512]{1,0:T(8,128)(2,1)} %refs_0_.1, f32[26,512]{1,0:T(8,128)} %refs_1_.1), custom_call_target="tpu_custom_call" | custom-call | flops 53248 | bytes 212992 | tf_op jit(solution)/shard_map/pallas_call | solution.py:53
  2.6 10.4 %all-to-all-start = ((bf16[16,32,128]{2,1,0:T(8,128)(2,1)}), bf16[16,32,128]{2,1,0:T(8,128)(2,1)S(1)}, u32[]{:S(2)}, u32[]{:S(2)}) async-start(bf16[16,32,128]{2,1,0:T(8,128)(2,1)} %bitcast.14), calls=%async_computation | async-start | bytes 262144 | tf_op jit(solution)/shard_map/all_to_all | solution.py:169
  13.1 0.3 multiply_convert_fusion.table_ref
  13.3 0.0 copy-done.1
  13.3 0.0 copy-done
  13.4 1.5 %shard_map.46 = (bf16[256,1664]{1,0:T(8,128)(2,1)S(1)}, bf16[256,1664]{1,0:T(8,128)(2,1)}) custom-call(bf16[256,3328]{1,0:T(8,128)(2,1)S(1)} %copy-done, s32[1,3328]{1,0:T(1,128)S(1)} %reshape.18.bits_ref, bf16[256,256]{1,0:T(8,128)(2,1)S(1)} %multiply_convert_fusion.table_ref), custom_call_target="tpu_custom_call" | custom-call | flops 436207616 | bytes 3407872 | tf_op jit(solution)/shard_map/pallas_call | solution.py:123
  14.9 2.7 %collective-permute-start = (bf16[256,1664]{1,0:T(8,128)(2,1)S(1)}, bf16[256,1664]{1,0:T(8,128)(2,1)S(1)}, u32[]{:S(2)}, u32[]{:S(2)}) collective-permute-start(bf16[256,1664]{1,0:T(8,128)(2,1)S(1)} %get-tuple-element.8.refs_0_), channel_id=1, source_target_pairs={{0,128},{128,0},{256,384},{384,256},{1,129},{129,1},{257,385},{385... | collective-permute-start | bytes 2555912 | tf_op jit(solution)/shard_map/ppermute | solution.py:176
  17.6 3.0 %collective-permute-start.1 = (bf16[256,1664]{1,0:T(8,128)(2,1)}, bf16[256,1664]{1,0:T(8,128)(2,1)S(1)}, u32[]{:S(2)}, u32[]{:S(2)}) collective-permute-start(bf16[256,1664]{1,0:T(8,128)(2,1)} %get-tuple-element.9), channel_id=1, source_target_pairs={{0,256},{128,384},{256,0},{384,128},{1,257},{129,385},{257,1},{385... | collective-permute-start | bytes 2555912 | tf_op jit(solution)/shard_map/ppermute | solution.py:176
  20.7 4.7 %collective-permute-start.2 = (bf16[256,1664]{1,0:T(8,128)(2,1)}, bf16[256,1664]{1,0:T(8,128)(2,1)S(1)}, u32[]{:S(2)}, u32[]{:S(2)}) collective-permute-start(bf16[256,1664]{1,0:T(8,128)(2,1)} %get-tuple-element.9), channel_id=1, source_target_pairs={{0,384},{128,256},{256,128},{384,0},{1,385},{129,257},{257,129},{3... | collective-permute-start | bytes 2555912 | tf_op jit(solution)/shard_map/ppermute | solution.py:176
  25.3 0.0 all-to-all-done
  25.3 0.1 shard_map.48
  25.4 15.8 %all_to_all.15 = bf16[16,32,128]{2,1,0:T(8,128)(2,1)S(1)} all-to-all(bf16[16,32,128]{2,1,0:T(8,128)(2,1)S(1)} %bitcast.12), channel_id=1, replica_groups=mesh['x'=4,'y'=8,'z'=8,'core'=2] {'z','core'}, dimensions={0} | all-to-all | bytes 262144 | tf_op jit(solution)/shard_map/all_to_all | solution.py:179
  41.2 28.1 %all_gather.7.refs_4_ = bf16[8,416,128]{2,1,0:T(8,128)(2,1)S(1)} all-gather(bf16[1,416,128]{2,1,0:T(8,128)(2,1)S(1)} %bitcast.15), channel_id=1, replica_groups=mesh['x'=4,'y'=8,'z'=8,'core'=2] {'y'}, dimensions={0}, use_global_device_ids=true | all-gather | bytes 958464 | tf_op jit(solution)/shard_map/all_gather | solution.py:180
  69.2 0.0 collective-permute-done.refs_1_
  69.2 0.0 collective-permute-done.1.refs_2_
  69.2 0.0 collective-permute-done.2.refs_3_
  69.3 1.2 %shard_map.49 = bf16[4,256,256]{2,1,0:T(8,128)(2,1)S(1)} custom-call(bf16[256,1664]{1,0:T(8,128)(2,1)S(1)} %get-tuple-element.8.refs_0_, bf16[256,1664]{1,0:T(8,128)(2,1)S(1)} %collective-permute-done.refs_1_, bf16[256,1664]{1,0:T(8,128)(2,1)S(1)} %collective-permute-done.1.refs_2_, bf16[256,1664]{1,0:T(8,128)(2,1)S(1)} %collective-permute-done.2.refs_3_, ...), custom_call_target="tpu_custom_call" | custom-call | flops 872415232 | bytes 3407872 | tf_op jit(solution)/shard_map/pallas_call | solution.py:147
  70.4 22.7 %all_to_all.16 = bf16[64,16,256]{2,1,0:T(8,128)(2,1)S(1)} all-to-all(bf16[64,16,256]{2,1,0:T(8,128)(2,1)S(1)} %bitcast.10), channel_id=1, replica_groups=mesh['x'=4,'y'=8,'z'=8,'core'=2] {'x','z','core'}, dimensions={0} | all-to-all | bytes 1048576 | tf_op jit(solution)/shard_map/all_to_all | solution.py:184
  93.1 0.1 reduce
  93.2 0.6 pad_maximum_fusion
  (3 shorter events, 0.0 us)
Async XLA Ops:
  0.0 13.3 %copy-start.1 = (s32[3328]{0:T(1024)S(1)}, s32[3328]{0:T(1024)}, u32[]{:S(2)}) copy-start(s32[3328]{0:T(1024)} %param.7) | copy-start | bytes 39940
  0.0 13.3 %copy-start = (bf16[256,3328]{1,0:T(8,128)(2,1)S(1)}, bf16[256,3328]{1,0:T(8,128)(2,1)}, u32[]{:S(2)}) copy-start(bf16[256,3328]{1,0:T(8,128)(2,1)} %hidden_ref.1) | copy-start | bytes 5111812
  2.6 22.7 %all-to-all-start = ((bf16[16,32,128]{2,1,0:T(8,128)(2,1)}), bf16[16,32,128]{2,1,0:T(8,128)(2,1)S(1)}, u32[]{:S(2)}, u32[]{:S(2)}) async-start(bf16[16,32,128]{2,1,0:T(8,128)(2,1)} %bitcast.14), calls=%async_computation | async-start | bytes 262144 | tf_op jit(solution)/shard_map/all_to_all | solution.py:169
  14.9 54.3 %collective-permute-start = (bf16[256,1664]{1,0:T(8,128)(2,1)S(1)}, bf16[256,1664]{1,0:T(8,128)(2,1)S(1)}, u32[]{:S(2)}, u32[]{:S(2)}) collective-permute-start(bf16[256,1664]{1,0:T(8,128)(2,1)S(1)} %get-tuple-element.8.refs_0_), channel_id=1, source_target_pairs={{0,128},{128,0},{256,384},{384,256},{1,129},{129,1},{257,385},{385... | collective-permute-start | bytes 2555912 | tf_op jit(solution)/shard_map/ppermute | solution.py:176
  17.6 51.6 %collective-permute-start.1 = (bf16[256,1664]{1,0:T(8,128)(2,1)}, bf16[256,1664]{1,0:T(8,128)(2,1)S(1)}, u32[]{:S(2)}, u32[]{:S(2)}) collective-permute-start(bf16[256,1664]{1,0:T(8,128)(2,1)} %get-tuple-element.9), channel_id=1, source_target_pairs={{0,256},{128,384},{256,0},{384,128},{1,257},{129,385},{257,1},{385... | collective-permute-start | bytes 2555912 | tf_op jit(solution)/shard_map/ppermute | solution.py:176
  20.7 48.6 %collective-permute-start.2 = (bf16[256,1664]{1,0:T(8,128)(2,1)}, bf16[256,1664]{1,0:T(8,128)(2,1)S(1)}, u32[]{:S(2)}, u32[]{:S(2)}) collective-permute-start(bf16[256,1664]{1,0:T(8,128)(2,1)} %get-tuple-element.9), channel_id=1, source_target_pairs={{0,384},{128,256},{256,128},{384,0},{1,385},{129,257},{257,129},{3... | collective-permute-start | bytes 2555912 | tf_op jit(solution)/shard_map/ppermute | solution.py:176

commit v4 on v3

--- a/solution.py
+++ b/solution.py
@@ -27,21 +27,22 @@
     return pltpu.CompilerParams(vmem_limit_bytes=mib * 1024 * 1024)
 
 
-def weight_kernel(rows, padded, codes_ref, scales_ref, out_ref, code_vmem, sem):
+def weight_kernel(rows, padded, codes_ref, scales_ref, out_ref, code_vmem, scale_vmem, sem):
     x, y = lax.axis_index("x"), lax.axis_index("y")
     share = (x // SIDES) * lax.axis_size("y") + y
     low = pl.multiple_of((x % SIDES) * (2 * LANES), 2 * LANES)
-    copy = pltpu.make_async_copy(
-        codes_ref.at[pl.ds(pl.multiple_of(share * rows, STEP), rows), pl.ds(low, 2 * LANES)],
-        code_vmem,
-        sem,
-    )
-    copy.start()
+    columns = pl.ds(low, 2 * LANES)
+    code_rows = pl.ds(pl.multiple_of(share * rows, STEP), rows)
+    code_copy = pltpu.make_async_copy(codes_ref.at[code_rows, columns], code_vmem, sem.at[0])
+    scale_copy = pltpu.make_async_copy(scales_ref.at[:, columns], scale_vmem, sem.at[1])
+    code_copy.start()
+    scale_copy.start()
     out_ref[2 * rows :] = jnp.zeros((padded - 2 * rows, LANES), BF16)
-    copy.wait()
+    code_copy.wait()
+    scale_copy.wait()
     for step in range(rows // STEP):
         group = (share * (rows // STEP) + step) // (GROUP // STEP)
-        scale = scales_ref[pl.ds(group, 1), pl.ds(low, 2 * LANES)]
+        scale = scale_vmem[pl.ds(group, 1)]
         value = code_vmem[step * STEP : (step + 1) * STEP].astype(F32) * scale
         value = value.astype(BF16)
         for side in range(2):
@@ -53,11 +54,12 @@
     return pl.pallas_call(
         lambda *refs: weight_kernel(rows, padded, *refs),
         out_shape=jax.ShapeDtypeStruct((padded, LANES), BF16),
-        in_specs=[
-            pl.BlockSpec(memory_space=pl.ANY),
-            pl.BlockSpec(memory_space=pltpu.VMEM),
+        in_specs=[pl.BlockSpec(memory_space=pl.ANY)] * 2,
+        scratch_shapes=[
+            pltpu.VMEM((rows, 2 * LANES), BF16),
+            pltpu.VMEM((scales.shape[0], 2 * LANES), F32),
+            pltpu.SemaphoreType.DMA((2,)),
         ],
-        scratch_shapes=[pltpu.VMEM((rows, 2 * LANES), BF16), pltpu.SemaphoreType.DMA],
         cost_estimate=pl.CostEstimate(
             flops=2 * rows * LANES, bytes_accessed=8 * rows * LANES, transcendentals=0
         ),
@@ -96,9 +98,12 @@
     )(parts)
 
 
-def turn_kernel(hidden_ref, bits_ref, table_ref, same_ref, other_ref):
+def turn_kernel(wanted, hidden_ref, bits_ref, table_ref, *out_refs):
     rows, width = hidden_ref.shape
     half = width // PARTS
+    cores = lax.axis_size("core")
+    chips = lax.axis_size("z")
+    run = rows // (chips * cores)
     own = lax.axis_index("x") // SIDES
     table = table_ref[...]
     for keep in range(PARTS):
@@ -106,23 +111,34 @@
         @pl.when(own == keep)
         def _(keep=keep):
             for low in range(0, width, TURN):
+                spots = [divmod(at, half) for at in range(low, low + TURN, LANES)]
+                if not any((part != keep) in wanted for part, _ in spots):
+                    continue
                 hidden = hidden_ref[:, low : low + TURN]
                 plus = bits_ref[:, low : low + TURN] == 1
                 signed = hidden * jnp.where(plus, 1.0, -1.0).astype(BF16)
                 turned = jnp.dot(signed, table, preferred_element_type=F32).astype(BF16)
-                for piece in range(0, TURN, LANES):
-                    part, inside = divmod(low + piece, half)
-                    out_ref = same_ref if part == keep else other_ref
-                    out_ref[:, inside : inside + LANES] = turned[:, piece : piece + LANES]
-
-
-def turn(hidden, sign_bits):
+                for piece, (part, inside) in enumerate(spots):
+                    if (part != keep) not in wanted:
+                        continue
+                    out_ref = out_refs[wanted.index(part != keep)]
+                    value = turned[:, piece * LANES : (piece + 1) * LANES]
+                    for chip in range(chips):
+                        for core in range(cores):
+                            source = (chip * cores + core) * run
+                            target = (core * chips + chip) * run
+                            out_ref[target : target + run, inside : inside + LANES] = value[
+                                source : source + run
+                            ]
+
+
+def turn(hidden, sign_bits, wanted):
     rows, width = hidden.shape
     table = (sylvester(TURN) * (1.0 / 16.0)).astype(BF16)
     half = jax.ShapeDtypeStruct((rows, width // PARTS), BF16)
     return pl.pallas_call(
-        turn_kernel,
-        out_shape=(half, half),
+        lambda *refs: turn_kernel(wanted, *refs),
+        out_shape=[half for _ in wanted],
         cost_estimate=pl.CostEstimate(
             flops=2 * rows * width * TURN, bytes_accessed=4 * rows * width, transcendentals=0
         ),
@@ -130,31 +146,39 @@
     )(hidden, sign_bits.reshape(1, width), table)
 
 
-def project_kernel(rows, act0, act1, act2, act3, mixed_ref, out_ref, weight_vmem):
+def project_kernel(rows, give, act0, act1, act2, act3, mixed_ref, out_ref, weight_vmem):
     for y in range(mixed_ref.shape[0]):
         for side in range(2):
             weight_vmem[y * rows : (y + 1) * rows, side * LANES : (side + 1) * LANES] = mixed_ref[
                 y, side * rows : (side + 1) * rows
             ]
-    x = lax.axis_index("x")
+    x, core = lax.axis_index("x"), lax.axis_index("core")
+    count = out_ref.shape[1]
+    spot = pl.ds(pl.multiple_of(jnp.bitwise_xor(core, give) * count, count), count)
     for flip, act_ref in enumerate((act0, act1, act2, act3)):
-        value = jnp.dot(act_ref[...], weight_vmem[...], preferred_element_type=F32)
-        out_ref[jnp.bitwise_xor(x, flip)] = value.astype(BF16)
-
-
-def project(acts, mixed, rows):
+        value = jnp.dot(act_ref[spot], weight_vmem[...], preferred_element_type=F32)
+        out_ref[jnp.bitwise_xor(x, flip)] = value.astype(out_ref.dtype)
+
+
+def project(acts, mixed, rows, give):
     count, half = acts[0].shape
     return pl.pallas_call(
-        lambda *refs: project_kernel(rows, *refs),
-        out_shape=jax.ShapeDtypeStruct((len(acts), count, 2 * LANES), BF16),
+        lambda *refs: project_kernel(rows, give, *refs),
+        out_shape=jax.ShapeDtypeStruct(
+            (len(acts), count // 2, 2 * LANES), BF16 if give else F32
+        ),
         scratch_shapes=[pltpu.VMEM((half, 2 * LANES), BF16)],
         cost_estimate=pl.CostEstimate(
-            flops=len(acts) * 4 * count * half * LANES,
-            bytes_accessed=len(acts) * 2 * count * half,
+            flops=len(acts) * 2 * count * half * LANES,
+            bytes_accessed=len(acts) * count * half,
             transcendentals=0,
         ),
         compiler_params=params(24),
     )(*acts, mixed)
+
+
+def swap(block, flip):
+    return lax.ppermute(block, "x", [(x, x ^ flip) for x in range(lax.axis_size("x"))])
 
 
 def per_device(hidden, codes, scales, sign_bits):
@@ -168,23 +192,23 @@
     pieces = weight.reshape(tp_count, padded // tp_count, LANES)
     pieces = lax.all_to_all(pieces, ("z", "core"), 0, 0, tiled=True)
 
-    same, other = turn(hidden, sign_bits)
+    same, other = turn(hidden, sign_bits, [0, 1])
     pieces = lax.optimization_barrier((pieces, same, other))[0]
-    acts = [same]
-    for flip in range(1, x_count):
-        route = [(x, x ^ flip) for x in range(x_count)]
-        acts.append(lax.ppermute(same if flip < SIDES else other, "x", route))
+    beside, across, corner = swap(same, 1), swap(other, SIDES), swap(other, SIDES + 1)
 
     mixed = mix(pieces.reshape(padded, LANES), tp_count, 1)
     mixed = lax.all_to_all(mixed[0], ("z", "core"), 0, 0, tiled=True)
     mixed = lax.all_gather(mixed.reshape(padded, LANES)[: 2 * rows], "y")
 
-    part_sum = project(acts, mixed, rows)
+    acts = [same, beside, across, corner]
+    give = project(acts, mixed, rows, 1)
+    got = lax.ppermute(give, "core", [(0, 1), (1, 0)])
+    chip_sum = (project(acts, mixed, rows, 0) + got.astype(F32)).astype(BF16)
     out_rows = row_count // tp_count
-    parts = lax.all_to_all(
-        part_sum.reshape(x_count * tp_count, out_rows, 2 * LANES), ("x", "z", "core"), 0, 0, tiled=True
-    )
-    parts = parts.reshape(PARTS, SIDES, tp_count, out_rows, 2 * LANES).astype(F32)
+    blocks = x_count * lax.axis_size("z")
+    parts = chip_sum.reshape(blocks, out_rows, 2 * LANES)
+    parts = lax.all_to_all(parts, ("x", "z"), 0, 0, tiled=True)
+    parts = parts.reshape(PARTS, SIDES, -1, out_rows, 2 * LANES).astype(F32)
     total = jnp.sum(parts, axis=(0, 2))
     return jnp.concatenate([total[side] for side in range(SIDES)], axis=-1).astype(BF16)
 

time: 95.6 us -> 90.8 us (0.950)
  blocking collectives: 66.5 us -> 60.5 us
  starting transfers between devices: 20.8 us -> 22.2 us
    all_to_all x1, blocking collectives: 22.7 us -> 16.7 us  [per_device(): parts = lax.all_to_all(parts, ('x', 'z'), 0, 0, tiled=True)]
    ppermute x3 -> x4, starting transfers between devices: 10.4 us -> 11.7 us  [the longest x3 9.81 us: swap(): lax.ppermute(block, 'x', [(x, x ^ flip) for x in range(lax.axis_size('x'))])]
    pallas_call x2 -> x3, Pallas kernels: 2.7 us -> 2.88 us  [the longest x1 1.55 us: turn(): pl.pallas_call(lambda *refs: turn_kernel(wanted, *refs), out_shape=[half...]
  transfers between devices with their start and end apart: 4 -> 5, of which waited for: 0 -> 1; matrix products, arithmetic and copies ran while one was open for 0% -> 0% of each run, Pallas kernels for 2% -> 3%
where the time goes in v4:
time: 90.8 us; the launch traced here: 89.3 us
  blocking collectives  60.5 us (67%)
  starting transfers between devices  22.2 us (24%)
  Pallas kernels  4.71 us (5%)
  other arithmetic  0.97 us (1%)
    all_gather x1, blocking collectives, per_device(): mixed = lax.all_gather(mixed.reshape(padded, LANES)[:2 * rows], 'y')  28.1 us
    all_to_all x1, blocking collectives, per_device(): parts = lax.all_to_all(parts, ('x', 'z'), 0, 0, tiled=True)  16.7 us
    all_to_all x1, blocking collectives, per_device(): mixed = lax.all_to_all(mixed[0], ('z', 'core'), 0, 0, tiled=True)  15.8 us
    all_to_all x1, starting transfers between devices, per_device(): pieces = lax.all_to_all(pieces, ('z', 'core'), 0, 0, tiled=True)  10.4 us
    ppermute x3, starting transfers between devices, swap(): lax.ppermute(block, 'x', [(x, x ^ flip) for x in range(lax.axis_size('x'))])  9.81 us
    ppermute x1, starting transfers between devices, per_device(): got = lax.ppermute(give, 'core', [(0, 1), (1, 0)])  1.92 us
  transfers between devices with their start and end apart: 5, of which 1 were waited for; matrix products, arithmetic and copies ran while one was open for 0% of the time, Pallas kernels for 3%

profile of v4, /device:TPU:6, one launch (start us, length us, event | category | flops | bytes accessed | tf_op | source)
XLA Modules:
  0.0 89.3 jit_solution(15438316106882355377)
XLA Ops:
  0.0 0.0 copy-start.1
  0.0 1.8 %shard_map.47 = bf16[512,128]{1,0:T(8,128)(2,1)} custom-call(bf16[3328,512]{1,0:T(8,128)(2,1)} %refs_0_.3, f32[26,512]{1,0:T(8,128)} %refs_1_.1), custom_call_target="tpu_custom_call" | custom-call | flops 53248 | bytes 212992 | tf_op jit(solution)/shard_map/pallas_call | solution.py:54
  1.8 10.4 %all-to-all-start = ((bf16[16,32,128]{2,1,0:T(8,128)(2,1)}), bf16[16,32,128]{2,1,0:T(8,128)(2,1)S(1)}, u32[]{:S(2)}, u32[]{:S(2)}) async-start(bf16[16,32,128]{2,1,0:T(8,128)(2,1)} %bitcast.14), calls=%async_computation | async-start | bytes 262144 | tf_op jit(solution)/shard_map/all_to_all | solution.py:193
  12.2 0.3 multiply_convert_fusion.refs_2_
  12.5 0.0 copy-done.1
  12.5 0.0 copy-done
  12.5 1.6 %shard_map.46 = (bf16[256,1664]{1,0:T(8,128)(2,1)S(1)}, bf16[256,1664]{1,0:T(8,128)(2,1)}) custom-call(bf16[256,3328]{1,0:T(8,128)(2,1)S(1)} %copy-done, s32[1,3328]{1,0:T(1,128)S(1)} %reshape.18.refs_1_, bf16[256,256]{1,0:T(8,128)(2,1)S(1)} %multiply_convert_fusion.refs_2_), custom_call_target="tpu_custom_call" | custom-call | flops 436207616 | bytes 3407872 | tf_op jit(solution)/shard_map/pallas_call | solution.py:139
  14.1 2.4 %collective-permute-start.2 = (bf16[256,1664]{1,0:T(8,128)(2,1)}, bf16[256,1664]{1,0:T(8,128)(2,1)S(1)}, u32[]{:S(2)}, u32[]{:S(2)}) collective-permute-start(bf16[256,1664]{1,0:T(8,128)(2,1)} %get-tuple-element.9), channel_id=1, source_target_pairs={{0,384},{128,256},{256,128},{384,0},{1,385},{129,257},{257,129},{3... | collective-permute-start | bytes 2555912 | tf_op jit(solution)/shard_map/ppermute | solution.py:181
  16.5 4.3 %collective-permute-start.1 = (bf16[256,1664]{1,0:T(8,128)(2,1)}, bf16[256,1664]{1,0:T(8,128)(2,1)S(1)}, u32[]{:S(2)}, u32[]{:S(2)}) collective-permute-start(bf16[256,1664]{1,0:T(8,128)(2,1)} %get-tuple-element.9), channel_id=1, source_target_pairs={{0,256},{128,384},{256,0},{384,128},{1,257},{129,385},{257,1},{385... | collective-permute-start | bytes 2555912 | tf_op jit(solution)/shard_map/ppermute | solution.py:181
  20.8 3.1 %collective-permute-start = (bf16[256,1664]{1,0:T(8,128)(2,1)S(1)}, bf16[256,1664]{1,0:T(8,128)(2,1)S(1)}, u32[]{:S(2)}, u32[]{:S(2)}) collective-permute-start(bf16[256,1664]{1,0:T(8,128)(2,1)S(1)} %get-tuple-element.8.refs_0_), channel_id=1, source_target_pairs={{0,128},{128,0},{256,384},{384,256},{1,129},{129,1},{257,385},{385... | collective-permute-start | bytes 2555912 | tf_op jit(solution)/shard_map/ppermute | solution.py:181
  23.9 0.0 all-to-all-done
  23.9 0.1 shard_map.48
  24.0 15.8 %all_to_all.15 = bf16[16,32,128]{2,1,0:T(8,128)(2,1)S(1)} all-to-all(bf16[16,32,128]{2,1,0:T(8,128)(2,1)S(1)} %bitcast.11), channel_id=1, replica_groups=mesh['x'=4,'y'=8,'z'=8,'core'=2] {'z','core'}, dimensions={0} | all-to-all | bytes 262144 | tf_op jit(solution)/shard_map/all_to_all | solution.py:200
  39.8 28.1 %all_gather.7.refs_4_ = bf16[8,416,128]{2,1,0:T(8,128)(2,1)S(1)} all-gather(bf16[1,416,128]{2,1,0:T(8,128)(2,1)S(1)} %bitcast.15), channel_id=1, replica_groups=mesh['x'=4,'y'=8,'z'=8,'core'=2] {'y'}, dimensions={0}, use_global_device_ids=true | all-gather | bytes 958464 | tf_op jit(solution)/shard_map/all_gather | solution.py:201
  67.8 0.0 collective-permute-done.2.refs_3_
  67.8 0.0 collective-permute-done.1.refs_2_
  67.8 0.0 collective-permute-done.refs_1_
  67.8 0.7 shard_map.50
  68.5 1.9 %collective-permute-start.3 = (bf16[4,128,256]{2,1,0:T(8,128)(2,1)S(1)}, bf16[4,128,256]{2,1,0:T(8,128)(2,1)S(1)}, u32[]{:S(2)}, u32[]{:S(2)}) collective-permute-start(bf16[4,128,256]{2,1,0:T(8,128)(2,1)S(1)} %shard_map.50), channel_id=1, source_target_pairs={{0,1},{1,0},{2,3},{3,2},{4,5},{5,4},{6,7},{7,6},{8,9},{9,8},{10,11... | collective-permute-start | bytes 786440 | tf_op jit(solution)/shard_map/ppermute | solution.py:205
  70.4 0.7 shard_map.49
  71.1 0.8 collective-permute-done.3
  71.9 0.1 add_convert_fusion
  72.0 16.7 %all_to_all.16 = bf16[32,16,256]{2,1,0:T(8,128)(2,1)S(1)} all-to-all(bf16[32,16,256]{2,1,0:T(8,128)(2,1)S(1)} %bitcast.13), channel_id=1, replica_groups=mesh['x'=4,'y'=8,'z'=8,'core'=2] {'x','z'}, dimensions={0} | all-to-all | bytes 524288 | tf_op jit(solution)/shard_map/all_to_all | solution.py:210
  88.7 0.6 pad_maximum_fusion
  (5 shorter events, 0.1 us)
Async XLA Ops:
  0.0 12.5 %copy-start.1 = (s32[3328]{0:T(1024)S(1)}, s32[3328]{0:T(1024)}, u32[]{:S(2)}) copy-start(s32[3328]{0:T(1024)} %param.7) | copy-start | bytes 39940
  0.0 12.5 %copy-start = (bf16[256,3328]{1,0:T(8,128)(2,1)S(1)}, bf16[256,3328]{1,0:T(8,128)(2,1)}, u32[]{:S(2)}) copy-start(bf16[256,3328]{1,0:T(8,128)(2,1)} %refs_0_.2) | copy-start | bytes 5111812
  1.8 22.1 %all-to-all-start = ((bf16[16,32,128]{2,1,0:T(8,128)(2,1)}), bf16[16,32,128]{2,1,0:T(8,128)(2,1)S(1)}, u32[]{:S(2)}, u32[]{:S(2)}) async-start(bf16[16,32,128]{2,1,0:T(8,128)(2,1)} %bitcast.14), calls=%async_computation | async-start | bytes 262144 | tf_op jit(solution)/shard_map/all_to_all | solution.py:193
  14.1 53.7 %collective-permute-start.2 = (bf16[256,1664]{1,0:T(8,128)(2,1)}, bf16[256,1664]{1,0:T(8,128)(2,1)S(1)}, u32[]{:S(2)}, u32[]{:S(2)}) collective-permute-start(bf16[256,1664]{1,0:T(8,128)(2,1)} %get-tuple-element.9), channel_id=1, source_target_pairs={{0,384},{128,256},{256,128},{384,0},{1,385},{129,257},{257,129},{3... | collective-permute-start | bytes 2555912 | tf_op jit(solution)/shard_map/ppermute | solution.py:181
  16.5 51.4 %collective-permute-start.1 = (bf16[256,1664]{1,0:T(8,128)(2,1)}, bf16[256,1664]{1,0:T(8,128)(2,1)S(1)}, u32[]{:S(2)}, u32[]{:S(2)}) collective-permute-start(bf16[256,1664]{1,0:T(8,128)(2,1)} %get-tuple-element.9), channel_id=1, source_target_pairs={{0,256},{128,384},{256,0},{384,128},{1,257},{129,385},{257,1},{385... | collective-permute-start | bytes 2555912 | tf_op jit(solution)/shard_map/ppermute | solution.py:181
  20.8 47.0 %collective-permute-start = (bf16[256,1664]{1,0:T(8,128)(2,1)S(1)}, bf16[256,1664]{1,0:T(8,128)(2,1)S(1)}, u32[]{:S(2)}, u32[]{:S(2)}) collective-permute-start(bf16[256,1664]{1,0:T(8,128)(2,1)S(1)} %get-tuple-element.8.refs_0_), channel_id=1, source_target_pairs={{0,128},{128,0},{256,384},{384,256},{1,129},{129,1},{257,385},{385... | collective-permute-start | bytes 2555912 | tf_op jit(solution)/shard_map/ppermute | solution.py:181
  68.5 3.4 %collective-permute-start.3 = (bf16[4,128,256]{2,1,0:T(8,128)(2,1)S(1)}, bf16[4,128,256]{2,1,0:T(8,128)(2,1)S(1)}, u32[]{:S(2)}, u32[]{:S(2)}) collective-permute-start(bf16[4,128,256]{2,1,0:T(8,128)(2,1)S(1)} %shard_map.50), channel_id=1, source_target_pairs={{0,1},{1,0},{2,3},{3,2},{4,5},{5,4},{6,7},{7,6},{8,9},{9,8},{10,11... | collective-permute-start | bytes 786440 | tf_op jit(solution)/shard_map/ppermute | solution.py:205

commit v5 on v4

v5 whole, which is shorter than its diff:
```python
import jax
import jax.numpy as jnp
from jax import lax
from jax.experimental import pallas as pl
from jax.experimental.pallas import tpu as pltpu
from jax.sharding import Mesh, PartitionSpec as P

BF16 = jnp.bfloat16
F32 = jnp.float32
TURN = 256
GROUP = 128
LANES = 128
STEP = 16
CORES = 2
PARTS, SIDES = 2, 2


def sylvester(matrix_size):
    indices = jnp.arange(matrix_size, dtype=jnp.int32)
    common = jnp.bitwise_and(indices[:, None], indices[None, :])
    parity = jnp.zeros((matrix_size, matrix_size), jnp.int32)
    for place in range(matrix_size.bit_length() - 1):
        parity = parity + jnp.bitwise_and(jnp.right_shift(common, place), 1)
    return 1.0 - 2.0 * jnp.bitwise_and(parity, 1).astype(F32)


def params(mib):
    return pltpu.CompilerParams(vmem_limit_bytes=mib * 1024 * 1024)


def weight_kernel(rows, padded, codes_ref, scales_ref, out_ref, code_vmem, scale_vmem, sem):
    x, far, near = (lax.axis_index(name) for name in ("x", "far", "near"))
    share = ((x // SIDES) * lax.axis_size("far") + far) * lax.axis_size("near") + near
    low = pl.multiple_of((x % SIDES) * (2 * LANES), 2 * LANES)
    columns = pl.ds(low, 2 * LANES)
    code_rows = pl.ds(pl.multiple_of(share * rows, STEP), rows)
    code_copy = pltpu.make_async_copy(codes_ref.at[code_rows, columns], code_vmem, sem.at[0])
    scale_copy = pltpu.make_async_copy(scales_ref.at[:, columns], scale_vmem, sem.at[1])
    code_copy.start()
    scale_copy.start()
    out_ref[2 * rows :] = jnp.zeros((padded - 2 * rows, LANES), BF16)
    code_copy.wait()
    scale_copy.wait()
    for step in range(rows // STEP):
        group = (share * (rows // STEP) + step) // (GROUP // STEP)
        scale = scale_vmem[pl.ds(group, 1)]
        value = code_vmem[step * STEP : (step + 1) * STEP].astype(F32) * scale
        value = value.astype(BF16)
        for side in range(2):
            at = side * rows + step * STEP
            out_ref[at : at + STEP] = value[:, side * LANES : (side + 1) * LANES]


def weight_share(codes, scales, rows, padded):
    return pl.pallas_call(
        lambda *refs: weight_kernel(rows, padded, *refs),
        out_shape=jax.ShapeDtypeStruct((padded, LANES), BF16),
        in_specs=[pl.BlockSpec(memory_space=pl.ANY)] * 2,
        scratch_shapes=[
            pltpu.VMEM((rows, 2 * LANES), BF16),
            pltpu.VMEM((scales.shape[0], 2 * LANES), F32),
            pltpu.SemaphoreType.DMA((2,)),
        ],
        cost_estimate=pl.CostEstimate(
            flops=2 * rows * LANES, bytes_accessed=8 * rows * LANES, transcendentals=0
        ),
        compiler_params=params(56),
    )(codes, scales)


def mix_kernel(count, in_ref, out_ref):
    rows = in_ref.shape[0] // count
    for low in range(0, rows, STEP):
        blocks = [
            in_ref[p * rows + low : p * rows + low + STEP].astype(F32) for p in range(count)
        ]
        stride = 1
        while stride < count:
            for p in range(count):
                if not p & stride:
                    a, b = blocks[p], blocks[p + stride]
                    blocks[p], blocks[p + stride] = a + b, a - b
            stride *= 2
        for q in range(count):
            value = (blocks[q] * (count**-0.5)).astype(BF16)
            for y in range(out_ref.shape[0]):
                out_ref[y, q, low : low + STEP] = value


def mix(parts, tp_count, copies):
    rows = parts.shape[0] // tp_count
    return pl.pallas_call(
        lambda *refs: mix_kernel(tp_count, *refs),
        out_shape=jax.ShapeDtypeStruct((copies, tp_count, rows, LANES), BF16),
        cost_estimate=pl.CostEstimate(
            flops=8 * parts.size, bytes_accessed=20 * parts.size, transcendentals=0
        ),
        compiler_params=params(24),
    )(parts)


def turn_kernel(hidden_ref, bits_ref, table_ref, *out_refs):
    same_refs, other_ref = out_refs[:CORES], out_refs[CORES]
    rows, width = hidden_ref.shape
    half = width // PARTS
    chips = lax.axis_size("z")
    run = rows // (chips * CORES)
    own = lax.axis_index("x") // SIDES
    table = table_ref[...]
    for keep in range(PARTS):

        @pl.when(own == keep)
        def _(keep=keep):
            for low in range(0, width, TURN):
                plus = bits_ref[:, low : low + TURN] == 1
                sign = jnp.where(plus, 1.0, -1.0).astype(BF16)
                for core in range(CORES):
                    runs = [(chip * CORES + core) * run for chip in range(chips)]
                    hidden = [hidden_ref[at : at + run, low : low + TURN] for at in runs]
                    signed = jnp.concatenate(hidden) * sign
                    turned = jnp.dot(signed, table, preferred_element_type=F32).astype(BF16)
                    for piece in range(0, TURN, LANES):
                        part, inside = divmod(low + piece, half)
                        lanes = slice(inside, inside + LANES)
                        value = turned[:, piece : piece + LANES]
                        if part == keep:
                            same_refs[core][:, lanes] = value
                        else:
                            at = core * chips * run
                            other_ref[at : at + chips * run, lanes] = value


def turn(hidden, sign_bits):
    rows, width = hidden.shape
    table = (sylvester(TURN) * (1.0 / 16.0)).astype(BF16)
    whole = jax.ShapeDtypeStruct((rows, width // PARTS), BF16)
    block = jax.ShapeDtypeStruct((rows // CORES, width // PARTS), BF16)
    return pl.pallas_call(
        turn_kernel,
        out_shape=[block, block, whole],
        cost_estimate=pl.CostEstimate(
            flops=2 * rows * width * TURN, bytes_accessed=4 * rows * width, transcendentals=0
        ),
        compiler_params=params(24),
    )(hidden, sign_bits.reshape(1, width), table)


def project_kernel(rows, give, *refs):
    (*act_refs, mixed_ref, out_ref, weight_vmem) = refs
    for y in range(mixed_ref.shape[0]):
        for side in range(2):
            weight_vmem[y * rows : (y + 1) * rows, side * LANES : (side + 1) * LANES] = mixed_ref[
                y, side * rows : (side + 1) * rows
            ]
    same, beside, across, corner = act_refs[0:2], act_refs[2:4], act_refs[4], act_refs[5]
    x, core = lax.axis_index("x"), lax.axis_index("core")
    count = out_ref.shape[1]
    for half in range(CORES):

        @pl.when(jnp.bitwise_xor(core, give) == half)
        def _(half=half):
            at = slice(half * count, (half + 1) * count)
            acts = same[half][...], beside[half][...], across[at], corner[at]
            for flip, act in enumerate(acts):
                value = jnp.dot(act, weight_vmem[...], preferred_element_type=F32)
                out_ref[jnp.bitwise_xor(x, flip)] = value.astype(out_ref.dtype)


def project(acts, mixed, rows, give):
    count, half = acts[0].shape
    groups = PARTS * SIDES
    return pl.pallas_call(
        lambda *refs: project_kernel(rows, give, *refs),
        out_shape=jax.ShapeDtypeStruct((groups, count, 2 * LANES), BF16 if give else F32),
        scratch_shapes=[pltpu.VMEM((half, 2 * LANES), BF16)],
        cost_estimate=pl.CostEstimate(
            flops=groups * 4 * count * half * LANES,
            bytes_accessed=groups * 2 * count * half,
            transcendentals=0,
        ),
        compiler_params=params(24),
    )(*acts, mixed)


def total_kernel(parts_ref, out_ref):
    parts, sides, chips, _, width = parts_ref.shape
    for side in range(sides):
        total = None
        for part in range(parts):
            for chip in range(chips):
                value = parts_ref[part, side, chip].astype(F32)
                total = value if total is None else total + value
        out_ref[:, side * width : (side + 1) * width] = total.astype(BF16)


def total(parts):
    _, sides, _, rows, width = parts.shape
    return pl.pallas_call(
        total_kernel,
        out_shape=jax.ShapeDtypeStruct((rows, sides * width), BF16),
        cost_estimate=pl.CostEstimate(
            flops=parts.size, bytes_accessed=2 * parts.size, transcendentals=0
        ),
        compiler_params=params(24),
    )(parts)


def swap(block, flip):
    return lax.ppermute(block, "x", [(x, x ^ flip) for x in range(lax.axis_size("x"))])


def per_device(hidden, codes, scales, sign_bits):
    row_count, local_width = hidden.shape
    x_count, far_count = lax.axis_size("x"), lax.axis_size("far")
    tp_count = lax.axis_size("z") * lax.axis_size("core")
    rows = local_width // PARTS // (far_count * lax.axis_size("near"))
    padded = -(-2 * rows // (STEP * tp_count)) * STEP * tp_count

    weight = weight_share(codes, scales, rows, padded)
    pieces = weight.reshape(tp_count, padded // tp_count, LANES)
    pieces = lax.all_to_all(pieces, ("z", "core"), 0, 0, tiled=True)

    same0, same1, other = turn(hidden, sign_bits)
    pieces = lax.optimization_barrier((pieces, other))[0]
    across, corner = swap(other, SIDES), swap(other, SIDES + 1)
    beside = swap(same0, 1), swap(same1, 1)

    near_count = lax.axis_size("near")
    mixed = mix(pieces.reshape(padded, LANES), tp_count, near_count)
    mixed = mixed.reshape(near_count * tp_count, padded // tp_count, LANES)
    mixed = lax.all_to_all(mixed, ("near", "z", "core"), 0, 0, tiled=True)
    mixed = mixed.reshape(near_count, padded, LANES)[:, : 2 * rows]
    mixed = lax.all_gather(mixed, "far", tiled=True)

    acts = [same0, same1, *beside, across, corner]
    give = project(acts, mixed, rows, 1)
    got = lax.ppermute(give, "core", [(0, 1), (1, 0)])
    chip_sum = (project(acts, mixed, rows, 0) + got.astype(F32)).astype(BF16)
    out_rows = row_count // tp_count
    blocks = x_count * lax.axis_size("z")
    parts = chip_sum.reshape(blocks, out_rows, 2 * LANES)
    parts = lax.all_to_all(parts, ("x", "z"), 0, 0, tiled=True)
    return total(parts.reshape(PARTS, SIDES, -1, out_rows, 2 * LANES))


def solution(mesh):
    devices = mesh.devices.reshape(4, 4, 2, 8, 2)
    grid = Mesh(devices, ("x", "far", "near", "z", "core"))
    rep, tp = ("x", "far", "near"), ("z", "core")
    return jax.shard_map(
        per_device,
        mesh=grid,
        in_specs=(P(rep, tp), P(tp, None), P(tp, None), P(tp)),
        out_specs=P(rep + tp, None),
        check_vma=False,
    )
```

time: 90.8 us -> 88.6 us (0.976)
  the two profiles are of different devices: /device:TPU:6 before, /device:TPU:8 now
where the time goes in v5:
time: 88.6 us; the launch traced here: 88.1 us
  blocking collectives  39.3 us (44%)
  starting transfers between devices  34.9 us (39%)
  Pallas kernels  6.36 us (7%)
  waiting for transfers between devices  6.05 us (7%)
  local copies, waits for them, and re-layouts  0.97 us (1%)
    all_gather x1, blocking collectives, per_device(): mixed = lax.all_gather(mixed, 'far', tiled=True)  21.5 us
    all_to_all x1, blocking collectives, per_device(): parts = lax.all_to_all(parts, ('x', 'z'), 0, 0, tiled=True)  17.8 us
    ppermute x4, starting transfers between devices, swap(): lax.ppermute(block, 'x', [(x, x ^ flip) for x in range(lax.axis_size('x'))])  13.8 us
    all_to_all x1, starting transfers between devices, per_device(): pieces = lax.all_to_all(pieces, ('z', 'core'), 0, 0, tiled=True)  10.4 us
    all_to_all x1, starting transfers between devices, per_device(): mixed = lax.all_to_all(mixed, ('near', 'z', 'core'), 0, 0, tiled=True)  8.75 us
    all_to_all x1, waiting for transfers between devices, per_device(): mixed = lax.all_to_all(mixed, ('near', 'z', 'core'), 0, 0, tiled=True)  5.35 us
    ppermute x1, starting transfers between devices, per_device(): got = lax.ppermute(give, 'core', [(0, 1), (1, 0)])  1.92 us
  transfers between devices with their start and end apart: 7, of which 2 were waited for; matrix products, arithmetic and copies ran while one was open for 1% of the time, Pallas kernels for 4%

profile of v5, /device:TPU:8, one launch (start us, length us, event | category | flops | bytes accessed | tf_op | source)
XLA Modules:
  0.0 88.1 jit_solution(6872130839046220640)
XLA Ops:
  0.0 1.8 %shard_map.47 = bf16[512,128]{1,0:T(8,128)(2,1)} custom-call(bf16[3328,512]{1,0:T(8,128)(2,1)} %refs_0_.1, f32[26,512]{1,0:T(8,128)} %refs_1_.1), custom_call_target="tpu_custom_call" | custom-call | flops 53248 | bytes 212992 | tf_op jit(solution)/shard_map/pallas_call | solution.py:55
  1.8 10.4 %all-to-all-start = ((bf16[16,32,128]{2,1,0:T(8,128)(2,1)}), bf16[16,32,128]{2,1,0:T(8,128)(2,1)S(1)}, u32[]{:S(2)}, u32[]{:S(2)}) async-start(bf16[16,32,128]{2,1,0:T(8,128)(2,1)} %bitcast.9), calls=%async_computation | async-start | bytes 262144 | tf_op jit(solution)/shard_map/all_to_all | solution.py:221
  12.2 0.3 multiply_convert_fusion.table_ref
  12.5 1.6 %shard_map.46 = (bf16[128,1664]{1,0:T(8,128)(2,1)S(1)}, bf16[128,1664]{1,0:T(8,128)(2,1)S(1)}, bf16[256,1664]{1,0:T(8,128)(2,1)}) custom-call(bf16[256,3328]{1,0:T(8,128)(2,1)S(1)} %copy-done, s32[1,3328]{1,0:T(1,128)S(1)} %reshape.21.bits_ref, bf16[256,256]{1,0:T(8,128)(2,1)S(1)} %multiply_convert_fusion.table_ref), custom_call_target="tpu_custom_call" | custom-call | flops 436207616 | bytes 3407872 | tf_op jit(solution)/shard_map/pallas_call | solution.py:138
  14.1 4.9 %collective-permute-start.2 = (bf16[256,1664]{1,0:T(8,128)(2,1)}, bf16[256,1664]{1,0:T(8,128)(2,1)S(1)}, u32[]{:S(2)}, u32[]{:S(2)}) collective-permute-start(bf16[256,1664]{1,0:T(8,128)(2,1)} %get-tuple-element.11), channel_id=1, source_target_pairs={{0,256},{128,384},{256,0},{384,128},{1,257},{129,385},{257,1},{385... | collective-permute-start | bytes 2555912 | tf_op jit(solution)/shard_map/ppermute | solution.py:209
  19.0 3.1 %collective-permute-start.3 = (bf16[256,1664]{1,0:T(8,128)(2,1)}, bf16[256,1664]{1,0:T(8,128)(2,1)S(1)}, u32[]{:S(2)}, u32[]{:S(2)}) collective-permute-start(bf16[256,1664]{1,0:T(8,128)(2,1)} %get-tuple-element.11), channel_id=1, source_target_pairs={{0,384},{128,256},{256,128},{384,0},{1,385},{129,257},{257,129},{3... | collective-permute-start | bytes 2555912 | tf_op jit(solution)/shard_map/ppermute | solution.py:209
  22.1 0.0 all-to-all-done
  22.1 0.8 shard_map.48
  22.9 8.7 %all-to-all-start.1 = ((bf16[32,32,128]{2,1,0:T(8,128)(2,1)}), bf16[32,32,128]{2,1,0:T(8,128)(2,1)}, u32[]{:S(2)}, u32[]{:S(2)}) async-start(bf16[32,32,128]{2,1,0:T(8,128)(2,1)} %bitcast.2), calls=%async_computation.1 | async-start | bytes 524288 | tf_op jit(solution)/shard_map/all_to_all | solution.py:231
  31.6 1.9 %collective-permute-start = (bf16[128,1664]{1,0:T(8,128)(2,1)S(1)}, bf16[128,1664]{1,0:T(8,128)(2,1)S(1)}, u32[]{:S(2)}, u32[]{:S(2)}) collective-permute-start(bf16[128,1664]{1,0:T(8,128)(2,1)S(1)} %get-tuple-element.9.refs_0_), channel_id=1, source_target_pairs={{0,128},{128,0},{256,384},{384,256},{1,129},{129,1},{257,385},{385... | collective-permute-start | bytes 1277960 | tf_op jit(solution)/shard_map/ppermute | solution.py:209
  33.6 3.9 %collective-permute-start.1 = (bf16[128,1664]{1,0:T(8,128)(2,1)S(1)}, bf16[128,1664]{1,0:T(8,128)(2,1)S(1)}, u32[]{:S(2)}, u32[]{:S(2)}) collective-permute-start(bf16[128,1664]{1,0:T(8,128)(2,1)S(1)} %get-tuple-element.10.refs_1_), channel_id=1, source_target_pairs={{0,128},{128,0},{256,384},{384,256},{1,129},{129,1},{257,385},{385... | collective-permute-start | bytes 1277960 | tf_op jit(solution)/shard_map/ppermute | solution.py:209
  37.5 5.4 %all-to-all-done.1 = bf16[32,32,128]{2,1,0:T(8,128)(2,1)} async-done(((bf16[32,32,128]{2,1,0:T(8,128)(2,1)}), bf16[32,32,128]{2,1,0:T(8,128)(2,1)}, u32[]{:S(2)}, u32[]{:S(2)}) %all-to-all-start.1) | async-done | bytes 262176 | tf_op jit(solution)/shard_map/all_to_all | solution.py:231
  42.9 0.9 %slice.4 = bf16[2,416,128]{2,1,0:T(8,128)(2,1)S(1)} slice(bf16[2,512,128]{2,1,0:T(8,128)(2,1)} %bitcast.3), slice={[0:2], [0:416], [0:128]} | slice | bytes 425984 | tf_op jit(solution)/shard_map/slice | solution.py:232
  43.8 21.5 %all_gather.3.refs_6_ = bf16[8,416,128]{2,1,0:T(8,128)(2,1)S(1)} all-gather(bf16[2,416,128]{2,1,0:T(8,128)(2,1)S(1)} %slice.4), channel_id=1, replica_groups=mesh['x'=4,'far'=4,'near'=2,'z'=8,'core'=2] {'far'}, dimensions={0}, use_global_device_ids=true | all-gather | bytes 1064960 | tf_op jit(solution)/shard_map/all_gather | solution.py:233
  65.3 0.0 collective-permute-done.refs_2_
  65.3 0.0 collective-permute-done.1.refs_3_
  65.3 0.0 collective-permute-done.3.refs_5_
  65.3 0.8 shard_map.50
  66.2 1.9 %collective-permute-start.4 = (bf16[4,128,256]{2,1,0:T(8,128)(2,1)S(1)}, bf16[4,128,256]{2,1,0:T(8,128)(2,1)S(1)}, u32[]{:S(2)}, u32[]{:S(2)}) collective-permute-start(bf16[4,128,256]{2,1,0:T(8,128)(2,1)S(1)} %shard_map.50), channel_id=1, source_target_pairs={{0,1},{1,0},{2,3},{3,2},{4,5},{5,4},{6,7},{7,6},{8,9},{9,8},{10,11... | collective-permute-start | bytes 786440 | tf_op jit(solution)/shard_map/ppermute | solution.py:237
  68.1 0.8 shard_map.49
  68.9 0.7 collective-permute-done.4
  69.6 0.1 add_convert_fusion
  69.6 17.8 %all_to_all.15 = bf16[32,16,256]{2,1,0:T(8,128)(2,1)S(1)} all-to-all(bf16[32,16,256]{2,1,0:T(8,128)(2,1)S(1)} %bitcast.8), channel_id=1, replica_groups=mesh['x'=4,'far'=4,'near'=2,'z'=8,'core'=2] {'x','z'}, dimensions={0} | all-to-all | bytes 524288 | tf_op jit(solution)/shard_map/all_to_all | solution.py:242
  87.5 0.6 shard_map.51
  (6 shorter events, 0.0 us)
Async XLA Ops:
  0.0 12.2 %copy-start.1 = (s32[3328]{0:T(1024)S(1)}, s32[3328]{0:T(1024)}, u32[]{:S(2)}) copy-start(s32[3328]{0:T(1024)} %param.7) | copy-start | bytes 39940
  0.0 12.5 %copy-start = (bf16[256,3328]{1,0:T(8,128)(2,1)S(1)}, bf16[256,3328]{1,0:T(8,128)(2,1)}, u32[]{:S(2)}) copy-start(bf16[256,3328]{1,0:T(8,128)(2,1)} %hidden_ref.1) | copy-start | bytes 5111812
  1.8 20.3 %all-to-all-start = ((bf16[16,32,128]{2,1,0:T(8,128)(2,1)}), bf16[16,32,128]{2,1,0:T(8,128)(2,1)S(1)}, u32[]{:S(2)}, u32[]{:S(2)}) async-start(bf16[16,32,128]{2,1,0:T(8,128)(2,1)} %bitcast.9), calls=%async_computation | async-start | bytes 262144 | tf_op jit(solution)/shard_map/all_to_all | solution.py:221
  14.1 51.2 %collective-permute-start.2 = (bf16[256,1664]{1,0:T(8,128)(2,1)}, bf16[256,1664]{1,0:T(8,128)(2,1)S(1)}, u32[]{:S(2)}, u32[]{:S(2)}) collective-permute-start(bf16[256,1664]{1,0:T(8,128)(2,1)} %get-tuple-element.11), channel_id=1, source_target_pairs={{0,256},{128,384},{256,0},{384,128},{1,257},{129,385},{257,1},{385... | collective-permute-start | bytes 2555912 | tf_op jit(solution)/shard_map/ppermute | solution.py:209
  19.0 46.3 %collective-permute-start.3 = (bf16[256,1664]{1,0:T(8,128)(2,1)}, bf16[256,1664]{1,0:T(8,128)(2,1)S(1)}, u32[]{:S(2)}, u32[]{:S(2)}) collective-permute-start(bf16[256,1664]{1,0:T(8,128)(2,1)} %get-tuple-element.11), channel_id=1, source_target_pairs={{0,384},{128,256},{256,128},{384,0},{1,385},{129,257},{257,129},{3... | collective-permute-start | bytes 2555912 | tf_op jit(solution)/shard_map/ppermute | solution.py:209
  22.9 20.0 %all-to-all-start.1 = ((bf16[32,32,128]{2,1,0:T(8,128)(2,1)}), bf16[32,32,128]{2,1,0:T(8,128)(2,1)}, u32[]{:S(2)}, u32[]{:S(2)}) async-start(bf16[32,32,128]{2,1,0:T(8,128)(2,1)} %bitcast.2), calls=%async_computation.1 | async-start | bytes 524288 | tf_op jit(solution)/shard_map/all_to_all | solution.py:231
  31.6 33.7 %collective-permute-start = (bf16[128,1664]{1,0:T(8,128)(2,1)S(1)}, bf16[128,1664]{1,0:T(8,128)(2,1)S(1)}, u32[]{:S(2)}, u32[]{:S(2)}) collective-permute-start(bf16[128,1664]{1,0:T(8,128)(2,1)S(1)} %get-tuple-element.9.refs_0_), channel_id=1, source_target_pairs={{0,128},{128,0},{256,384},{384,256},{1,129},{129,1},{257,385},{385... | collective-permute-start | bytes 1277960 | tf_op jit(solution)/shard_map/ppermute | solution.py:209
  33.6 31.7 %collective-permute-start.1 = (bf16[128,1664]{1,0:T(8,128)(2,1)S(1)}, bf16[128,1664]{1,0:T(8,128)(2,1)S(1)}, u32[]{:S(2)}, u32[]{:S(2)}) collective-permute-start(bf16[128,1664]{1,0:T(8,128)(2,1)S(1)} %get-tuple-element.10.refs_1_), channel_id=1, source_target_pairs={{0,128},{128,0},{256,384},{384,256},{1,129},{129,1},{257,385},{385... | collective-permute-start | bytes 1277960 | tf_op jit(solution)/shard_map/ppermute | solution.py:209
  66.2 3.4 %collective-permute-start.4 = (bf16[4,128,256]{2,1,0:T(8,128)(2,1)S(1)}, bf16[4,128,256]{2,1,0:T(8,128)(2,1)S(1)}, u32[]{:S(2)}, u32[]{:S(2)}) collective-permute-start(bf16[4,128,256]{2,1,0:T(8,128)(2,1)S(1)} %shard_map.50), channel_id=1, source_target_pairs={{0,1},{1,0},{2,3},{3,2},{4,5},{5,4},{6,7},{7,6},{8,9},{9,8},{10,11... | collective-permute-start | bytes 786440 | tf_op jit(solution)/shard_map/ppermute | solution.py:237

commit v6 on v5

--- a/solution.py
+++ b/solution.py
@@ -30,8 +30,8 @@
 
 def weight_kernel(rows, padded, codes_ref, scales_ref, out_ref, code_vmem, scale_vmem, sem):
     x, far, near = (lax.axis_index(name) for name in ("x", "far", "near"))
-    share = ((x // SIDES) * lax.axis_size("far") + far) * lax.axis_size("near") + near
-    low = pl.multiple_of((x % SIDES) * (2 * LANES), 2 * LANES)
+    share = ((x % PARTS) * lax.axis_size("far") + far) * lax.axis_size("near") + near
+    low = pl.multiple_of((x // PARTS) * (2 * LANES), 2 * LANES)
     columns = pl.ds(low, 2 * LANES)
     code_rows = pl.ds(pl.multiple_of(share * rows, STEP), rows)
     code_copy = pltpu.make_async_copy(codes_ref.at[code_rows, columns], code_vmem, sem.at[0])
@@ -105,7 +105,7 @@
     half = width // PARTS
     chips = lax.axis_size("z")
     run = rows // (chips * CORES)
-    own = lax.axis_index("x") // SIDES
+    own = lax.axis_index("x") % PARTS
     table = table_ref[...]
     for keep in range(PARTS):
 
@@ -152,7 +152,7 @@
             weight_vmem[y * rows : (y + 1) * rows, side * LANES : (side + 1) * LANES] = mixed_ref[
                 y, side * rows : (side + 1) * rows
             ]
-    same, beside, across, corner = act_refs[0:2], act_refs[2:4], act_refs[4], act_refs[5]
+    same, beside, across, corner = act_refs[0:2], act_refs[2], act_refs[3:5], act_refs[5]
     x, core = lax.axis_index("x"), lax.axis_index("core")
     count = out_ref.shape[1]
     for half in range(CORES):
@@ -160,7 +160,7 @@
         @pl.when(jnp.bitwise_xor(core, give) == half)
         def _(half=half):
             at = slice(half * count, (half + 1) * count)
-            acts = same[half][...], beside[half][...], across[at], corner[at]
+            acts = same[half][...], beside[at], across[half][...], corner[at]
             for flip, act in enumerate(acts):
                 value = jnp.dot(act, weight_vmem[...], preferred_element_type=F32)
                 out_ref[jnp.bitwise_xor(x, flip)] = value.astype(out_ref.dtype)
@@ -183,18 +183,18 @@
 
 
 def total_kernel(parts_ref, out_ref):
-    parts, sides, chips, _, width = parts_ref.shape
+    sides, parts, chips, _, width = parts_ref.shape
     for side in range(sides):
         total = None
         for part in range(parts):
             for chip in range(chips):
-                value = parts_ref[part, side, chip].astype(F32)
+                value = parts_ref[side, part, chip].astype(F32)
                 total = value if total is None else total + value
         out_ref[:, side * width : (side + 1) * width] = total.astype(BF16)
 
 
 def total(parts):
-    _, sides, _, rows, width = parts.shape
+    sides, _, _, rows, width = parts.shape
     return pl.pallas_call(
         total_kernel,
         out_shape=jax.ShapeDtypeStruct((rows, sides * width), BF16),
@@ -222,8 +222,8 @@
 
     same0, same1, other = turn(hidden, sign_bits)
     pieces = lax.optimization_barrier((pieces, other))[0]
-    across, corner = swap(other, SIDES), swap(other, SIDES + 1)
-    beside = swap(same0, 1), swap(same1, 1)
+    beside, corner = swap(other, 1), swap(other, PARTS + 1)
+    across = swap(same0, PARTS), swap(same1, PARTS)
 
     near_count = lax.axis_size("near")
     mixed = mix(pieces.reshape(padded, LANES), tp_count, near_count)
@@ -232,7 +232,7 @@
     mixed = mixed.reshape(near_count, padded, LANES)[:, : 2 * rows]
     mixed = lax.all_gather(mixed, "far", tiled=True)
 
-    acts = [same0, same1, *beside, across, corner]
+    acts = [same0, same1, beside, *across, corner]
     give = project(acts, mixed, rows, 1)
     got = lax.ppermute(give, "core", [(0, 1), (1, 0)])
     chip_sum = (project(acts, mixed, rows, 0) + got.astype(F32)).astype(BF16)
@@ -240,7 +240,7 @@
     blocks = x_count * lax.axis_size("z")
     parts = chip_sum.reshape(blocks, out_rows, 2 * LANES)
     parts = lax.all_to_all(parts, ("x", "z"), 0, 0, tiled=True)
-    return total(parts.reshape(PARTS, SIDES, -1, out_rows, 2 * LANES))
+    return total(parts.reshape(SIDES, PARTS, -1, out_rows, 2 * LANES))
 
 
 def solution(mesh):

time: 88.6 us -> 87 us (0.982)
  waiting for transfers between devices: 6.05 us -> 4.54 us
  blocking collectives: 39.3 us -> 38.3 us
  starting transfers between devices: 34.9 us -> 35.9 us
    all_to_all x1, waiting for transfers between devices: 5.35 us -> 3.85 us  [per_device(): mixed = lax.all_to_all(mixed, ('near', 'z', 'core'), 0, 0, tiled=True)]
    all_to_all x1, blocking collectives: 17.8 us -> 16.9 us  [per_device(): parts = lax.all_to_all(parts, ('x', 'z'), 0, 0, tiled=True)]
    ppermute x4, starting transfers between devices: 13.8 us -> 14.7 us  [swap(): lax.ppermute(block, 'x', [(x, x ^ flip) for x in range(lax.axis_size('x'))])]
where the time goes in v6:
time: 87 us; the launch traced here: 86.5 us
  blocking collectives  38.3 us (44%)
  starting transfers between devices  35.9 us (41%)
  Pallas kernels  6.36 us (7%)
  waiting for transfers between devices  4.54 us (5%)
  local copies, waits for them, and re-layouts  0.97 us (1%)
    all_gather x1, blocking collectives, per_device(): mixed = lax.all_gather(mixed, 'far', tiled=True)  21.5 us
    all_to_all x1, blocking collectives, per_device(): parts = lax.all_to_all(parts, ('x', 'z'), 0, 0, tiled=True)  16.9 us
    ppermute x4, starting transfers between devices, swap(): lax.ppermute(block, 'x', [(x, x ^ flip) for x in range(lax.axis_size('x'))])  14.7 us
    all_to_all x1, starting transfers between devices, per_device(): pieces = lax.all_to_all(pieces, ('z', 'core'), 0, 0, tiled=True)  10.4 us
    all_to_all x1, starting transfers between devices, per_device(): mixed = lax.all_to_all(mixed, ('near', 'z', 'core'), 0, 0, tiled=True)  8.78 us
    all_to_all x1, waiting for transfers between devices, per_device(): mixed = lax.all_to_all(mixed, ('near', 'z', 'core'), 0, 0, tiled=True)  3.85 us
    ppermute x1, starting transfers between devices, per_device(): got = lax.ppermute(give, 'core', [(0, 1), (1, 0)])  1.92 us
    pallas_call x1, Pallas kernels, weight_share(): pl.pallas_call(lambda *refs: weight_kernel(rows, padded, *refs), out_shap...  1.77 us
  transfers between devices with their start and end apart: 7, of which 2 were waited for; matrix products, arithmetic and copies ran while one was open for 1% of the time, Pallas kernels for 4%

profile of v6, /device:TPU:8, one launch (start us, length us, event | category | flops | bytes accessed | tf_op | source)
XLA Modules:
  0.0 86.5 jit_solution(7808649568703580957)
XLA Ops:
  0.0 1.8 %shard_map.47 = bf16[512,128]{1,0:T(8,128)(2,1)} custom-call(bf16[3328,512]{1,0:T(8,128)(2,1)} %refs_0_.1, f32[26,512]{1,0:T(8,128)} %refs_1_.1), custom_call_target="tpu_custom_call" | custom-call | flops 53248 | bytes 212992 | tf_op jit(solution)/shard_map/pallas_call | solution.py:55
  1.8 10.4 %all-to-all-start = ((bf16[16,32,128]{2,1,0:T(8,128)(2,1)}), bf16[16,32,128]{2,1,0:T(8,128)(2,1)S(1)}, u32[]{:S(2)}, u32[]{:S(2)}) async-start(bf16[16,32,128]{2,1,0:T(8,128)(2,1)} %bitcast.9), calls=%async_computation | async-start | bytes 262144 | tf_op jit(solution)/shard_map/all_to_all | solution.py:221
  12.2 0.3 multiply_convert_fusion.table_ref
  12.5 1.6 %shard_map.46 = (bf16[128,1664]{1,0:T(8,128)(2,1)S(1)}, bf16[128,1664]{1,0:T(8,128)(2,1)S(1)}, bf16[256,1664]{1,0:T(8,128)(2,1)}) custom-call(bf16[256,3328]{1,0:T(8,128)(2,1)S(1)} %copy-done, s32[1,3328]{1,0:T(1,128)S(1)} %reshape.21.bits_ref, bf16[256,256]{1,0:T(8,128)(2,1)S(1)} %multiply_convert_fusion.table_ref), custom_call_target="tpu_custom_call" | custom-call | flops 436207616 | bytes 3407872 | tf_op jit(solution)/shard_map/pallas_call | solution.py:138
  14.1 3.4 %collective-permute-start = (bf16[256,1664]{1,0:T(8,128)(2,1)}, bf16[256,1664]{1,0:T(8,128)(2,1)S(1)}, u32[]{:S(2)}, u32[]{:S(2)}) collective-permute-start(bf16[256,1664]{1,0:T(8,128)(2,1)} %get-tuple-element.11), channel_id=1, source_target_pairs={{0,128},{128,0},{256,384},{384,256},{1,129},{129,1},{257,385},{385... | collective-permute-start | bytes 2555912 | tf_op jit(solution)/shard_map/ppermute | solution.py:209
  17.5 4.0 %collective-permute-start.3 = (bf16[256,1664]{1,0:T(8,128)(2,1)}, bf16[256,1664]{1,0:T(8,128)(2,1)S(1)}, u32[]{:S(2)}, u32[]{:S(2)}) collective-permute-start(bf16[256,1664]{1,0:T(8,128)(2,1)} %get-tuple-element.11), channel_id=1, source_target_pairs={{0,384},{128,256},{256,128},{384,0},{1,385},{129,257},{257,129},{3... | collective-permute-start | bytes 2555912 | tf_op jit(solution)/shard_map/ppermute | solution.py:209
  21.5 0.0 all-to-all-done
  21.5 0.8 shard_map.48
  22.3 8.8 %all-to-all-start.1 = ((bf16[32,32,128]{2,1,0:T(8,128)(2,1)}), bf16[32,32,128]{2,1,0:T(8,128)(2,1)}, u32[]{:S(2)}, u32[]{:S(2)}) async-start(bf16[32,32,128]{2,1,0:T(8,128)(2,1)} %bitcast.2), calls=%async_computation.1 | async-start | bytes 524288 | tf_op jit(solution)/shard_map/all_to_all | solution.py:231
  31.1 2.6 %collective-permute-start.1 = (bf16[128,1664]{1,0:T(8,128)(2,1)S(1)}, bf16[128,1664]{1,0:T(8,128)(2,1)S(1)}, u32[]{:S(2)}, u32[]{:S(2)}) collective-permute-start(bf16[128,1664]{1,0:T(8,128)(2,1)S(1)} %get-tuple-element.9.refs_0_), channel_id=1, source_target_pairs={{0,256},{128,384},{256,0},{384,128},{1,257},{129,385},{257,1},{385... | collective-permute-start | bytes 1277960 | tf_op jit(solution)/shard_map/ppermute | solution.py:209
  33.6 4.8 %collective-permute-start.2 = (bf16[128,1664]{1,0:T(8,128)(2,1)S(1)}, bf16[128,1664]{1,0:T(8,128)(2,1)S(1)}, u32[]{:S(2)}, u32[]{:S(2)}) collective-permute-start(bf16[128,1664]{1,0:T(8,128)(2,1)S(1)} %get-tuple-element.10.refs_1_), channel_id=1, source_target_pairs={{0,256},{128,384},{256,0},{384,128},{1,257},{129,385},{257,1},{385... | collective-permute-start | bytes 1277960 | tf_op jit(solution)/shard_map/ppermute | solution.py:209
  38.4 3.8 %all-to-all-done.1 = bf16[32,32,128]{2,1,0:T(8,128)(2,1)} async-done(((bf16[32,32,128]{2,1,0:T(8,128)(2,1)}), bf16[32,32,128]{2,1,0:T(8,128)(2,1)}, u32[]{:S(2)}, u32[]{:S(2)}) %all-to-all-start.1) | async-done | bytes 262176 | tf_op jit(solution)/shard_map/all_to_all | solution.py:231
  42.3 0.9 %slice.4 = bf16[2,416,128]{2,1,0:T(8,128)(2,1)S(1)} slice(bf16[2,512,128]{2,1,0:T(8,128)(2,1)} %bitcast.3), slice={[0:2], [0:416], [0:128]} | slice | bytes 425984 | tf_op jit(solution)/shard_map/slice | solution.py:232
  43.2 21.5 %all_gather.3.refs_6_ = bf16[8,416,128]{2,1,0:T(8,128)(2,1)S(1)} all-gather(bf16[2,416,128]{2,1,0:T(8,128)(2,1)S(1)} %slice.4), channel_id=1, replica_groups=mesh['x'=4,'far'=4,'near'=2,'z'=8,'core'=2] {'far'}, dimensions={0}, use_global_device_ids=true | all-gather | bytes 1064960 | tf_op jit(solution)/shard_map/all_gather | solution.py:233
  64.7 0.0 collective-permute-done.1.refs_3_
  64.7 0.0 collective-permute-done.2.refs_4_
  64.7 0.0 collective-permute-done.refs_2_
  64.7 0.8 shard_map.50
  65.6 1.9 %collective-permute-start.4 = (bf16[4,128,256]{2,1,0:T(8,128)(2,1)S(1)}, bf16[4,128,256]{2,1,0:T(8,128)(2,1)S(1)}, u32[]{:S(2)}, u32[]{:S(2)}) collective-permute-start(bf16[4,128,256]{2,1,0:T(8,128)(2,1)S(1)} %shard_map.50), channel_id=1, source_target_pairs={{0,1},{1,0},{2,3},{3,2},{4,5},{5,4},{6,7},{7,6},{8,9},{9,8},{10,11... | collective-permute-start | bytes 786440 | tf_op jit(solution)/shard_map/ppermute | solution.py:237
  67.5 0.8 shard_map.49
  68.3 0.7 collective-permute-done.4
  69.0 0.1 add_convert_fusion
  69.0 16.9 %all_to_all.15 = bf16[32,16,256]{2,1,0:T(8,128)(2,1)S(1)} all-to-all(bf16[32,16,256]{2,1,0:T(8,128)(2,1)S(1)} %bitcast.8), channel_id=1, replica_groups=mesh['x'=4,'far'=4,'near'=2,'z'=8,'core'=2] {'x','z'}, dimensions={0} | all-to-all | bytes 524288 | tf_op jit(solution)/shard_map/all_to_all | solution.py:242
  85.9 0.6 shard_map.51
  (6 shorter events, 0.0 us)
Async XLA Ops:
  0.0 12.2 %copy-start.1 = (s32[3328]{0:T(1024)S(1)}, s32[3328]{0:T(1024)}, u32[]{:S(2)}) copy-start(s32[3328]{0:T(1024)} %param.7) | copy-start | bytes 39940
  0.0 12.5 %copy-start = (bf16[256,3328]{1,0:T(8,128)(2,1)S(1)}, bf16[256,3328]{1,0:T(8,128)(2,1)}, u32[]{:S(2)}) copy-start(bf16[256,3328]{1,0:T(8,128)(2,1)} %hidden_ref.1) | copy-start | bytes 5111812
  1.8 19.7 %all-to-all-start = ((bf16[16,32,128]{2,1,0:T(8,128)(2,1)}), bf16[16,32,128]{2,1,0:T(8,128)(2,1)S(1)}, u32[]{:S(2)}, u32[]{:S(2)}) async-start(bf16[16,32,128]{2,1,0:T(8,128)(2,1)} %bitcast.9), calls=%async_computation | async-start | bytes 262144 | tf_op jit(solution)/shard_map/all_to_all | solution.py:221
  14.1 50.7 %collective-permute-start = (bf16[256,1664]{1,0:T(8,128)(2,1)}, bf16[256,1664]{1,0:T(8,128)(2,1)S(1)}, u32[]{:S(2)}, u32[]{:S(2)}) collective-permute-start(bf16[256,1664]{1,0:T(8,128)(2,1)} %get-tuple-element.11), channel_id=1, source_target_pairs={{0,128},{128,0},{256,384},{384,256},{1,129},{129,1},{257,385},{385... | collective-permute-start | bytes 2555912 | tf_op jit(solution)/shard_map/ppermute | solution.py:209
  17.5 47.3 %collective-permute-start.3 = (bf16[256,1664]{1,0:T(8,128)(2,1)}, bf16[256,1664]{1,0:T(8,128)(2,1)S(1)}, u32[]{:S(2)}, u32[]{:S(2)}) collective-permute-start(bf16[256,1664]{1,0:T(8,128)(2,1)} %get-tuple-element.11), channel_id=1, source_target_pairs={{0,384},{128,256},{256,128},{384,0},{1,385},{129,257},{257,129},{3... | collective-permute-start | bytes 2555912 | tf_op jit(solution)/shard_map/ppermute | solution.py:209
  22.3 20.0 %all-to-all-start.1 = ((bf16[32,32,128]{2,1,0:T(8,128)(2,1)}), bf16[32,32,128]{2,1,0:T(8,128)(2,1)}, u32[]{:S(2)}, u32[]{:S(2)}) async-start(bf16[32,32,128]{2,1,0:T(8,128)(2,1)} %bitcast.2), calls=%async_computation.1 | async-start | bytes 524288 | tf_op jit(solution)/shard_map/all_to_all | solution.py:231
  31.1 33.7 %collective-permute-start.1 = (bf16[128,1664]{1,0:T(8,128)(2,1)S(1)}, bf16[128,1664]{1,0:T(8,128)(2,1)S(1)}, u32[]{:S(2)}, u32[]{:S(2)}) collective-permute-start(bf16[128,1664]{1,0:T(8,128)(2,1)S(1)} %get-tuple-element.9.refs_0_), channel_id=1, source_target_pairs={{0,256},{128,384},{256,0},{384,128},{1,257},{129,385},{257,1},{385... | collective-permute-start | bytes 1277960 | tf_op jit(solution)/shard_map/ppermute | solution.py:209
  33.6 31.1 %collective-permute-start.2 = (bf16[128,1664]{1,0:T(8,128)(2,1)S(1)}, bf16[128,1664]{1,0:T(8,128)(2,1)S(1)}, u32[]{:S(2)}, u32[]{:S(2)}) collective-permute-start(bf16[128,1664]{1,0:T(8,128)(2,1)S(1)} %get-tuple-element.10.refs_1_), channel_id=1, source_target_pairs={{0,256},{128,384},{256,0},{384,128},{1,257},{129,385},{257,1},{385... | collective-permute-start | bytes 1277960 | tf_op jit(solution)/shard_map/ppermute | solution.py:209
  65.6 3.4 %collective-permute-start.4 = (bf16[4,128,256]{2,1,0:T(8,128)(2,1)S(1)}, bf16[4,128,256]{2,1,0:T(8,128)(2,1)S(1)}, u32[]{:S(2)}, u32[]{:S(2)}) collective-permute-start(bf16[4,128,256]{2,1,0:T(8,128)(2,1)S(1)} %shard_map.50), channel_id=1, source_target_pairs={{0,1},{1,0},{2,3},{3,2},{4,5},{5,4},{6,7},{7,6},{8,9},{9,8},{10,11... | collective-permute-start | bytes 786440 | tf_op jit(solution)/shard_map/ppermute | solution.py:237

commit v7 on v6

--- a/solution.py
+++ b/solution.py
@@ -99,8 +99,8 @@
     )(parts)
 
 
-def turn_kernel(hidden_ref, bits_ref, table_ref, *out_refs):
-    same_refs, other_ref = out_refs[:CORES], out_refs[CORES]
+def turn_kernel(hidden_ref, bits_ref, table_ref, *refs):
+    same_refs, (other_ref, other_vmem, sems) = refs[:CORES], refs[CORES:]
     rows, width = hidden_ref.shape
     half = width // PARTS
     chips = lax.axis_size("z")
@@ -111,7 +111,9 @@
 
         @pl.when(own == keep)
         def _(keep=keep):
-            for low in range(0, width, TURN):
+            copies = []
+            blocks = list(range(0, width, TURN))
+            for low in blocks if keep == PARTS - 1 else blocks[::-1]:
                 plus = bits_ref[:, low : low + TURN] == 1
                 sign = jnp.where(plus, 1.0, -1.0).astype(BF16)
                 for core in range(CORES):
@@ -127,7 +129,18 @@
                             same_refs[core][:, lanes] = value
                         else:
                             at = core * chips * run
-                            other_ref[at : at + chips * run, lanes] = value
+                            other_vmem[at : at + chips * run, lanes] = value
+                for piece in range(0, TURN, LANES):
+                    part, inside = divmod(low + piece, half)
+                    if part != keep:
+                        lanes = pl.ds(inside, LANES)
+                        copy = pltpu.make_async_copy(
+                            other_vmem.at[:, lanes], other_ref.at[:, lanes], sems.at[inside // LANES]
+                        )
+                        copy.start()
+                        copies.append(copy)
+            for copy in copies:
+                copy.wait()
 
 
 def turn(hidden, sign_bits):
@@ -135,9 +148,15 @@
     table = (sylvester(TURN) * (1.0 / 16.0)).astype(BF16)
     whole = jax.ShapeDtypeStruct((rows, width // PARTS), BF16)
     block = jax.ShapeDtypeStruct((rows // CORES, width // PARTS), BF16)
+    vmem = pl.BlockSpec(memory_space=pltpu.VMEM)
     return pl.pallas_call(
         turn_kernel,
         out_shape=[block, block, whole],
+        out_specs=[vmem, vmem, pl.BlockSpec(memory_space=pl.ANY)],
+        scratch_shapes=[
+            pltpu.VMEM(whole.shape, BF16),
+            pltpu.SemaphoreType.DMA((width // PARTS // LANES,)),
+        ],
         cost_estimate=pl.CostEstimate(
             flops=2 * rows * width * TURN, bytes_accessed=4 * rows * width, transcendentals=0
         ),

time: 87 us -> 86.8 us (level)
  transfers between devices with their start and end apart: 7 -> 7, of which waited for: 2 -> 2; matrix products, arithmetic and copies ran while one was open for 1% -> 1% of each run, Pallas kernels for 4% -> 3%
where the time goes in v7:
time: 86.8 us; the launch traced here: 86.3 us
  blocking collectives  38.4 us (44%)
  starting transfers between devices  35.9 us (41%)
  Pallas kernels  6.07 us (7%)
  waiting for transfers between devices  4.55 us (5%)
  local copies, waits for them, and re-layouts  0.97 us (1%)
    all_gather x1, blocking collectives, per_device(): mixed = lax.all_gather(mixed, 'far', tiled=True)  21.5 us
    all_to_all x1, blocking collectives, per_device(): parts = lax.all_to_all(parts, ('x', 'z'), 0, 0, tiled=True)  16.9 us
    ppermute x4, starting transfers between devices, swap(): lax.ppermute(block, 'x', [(x, x ^ flip) for x in range(lax.axis_size('x'))])  14.8 us
    all_to_all x1, starting transfers between devices, per_device(): pieces = lax.all_to_all(pieces, ('z', 'core'), 0, 0, tiled=True)  10.4 us
    all_to_all x1, starting transfers between devices, per_device(): mixed = lax.all_to_all(mixed, ('near', 'z', 'core'), 0, 0, tiled=True)  8.75 us
    all_to_all x1, waiting for transfers between devices, per_device(): mixed = lax.all_to_all(mixed, ('near', 'z', 'core'), 0, 0, tiled=True)  3.85 us
    ppermute x1, starting transfers between devices, per_device(): got = lax.ppermute(give, 'core', [(0, 1), (1, 0)])  1.92 us
    pallas_call x1, Pallas kernels, weight_share(): pl.pallas_call(lambda *refs: weight_kernel(rows, padded, *refs), out_shap...  1.77 us
  transfers between devices with their start and end apart: 7, of which 2 were waited for; matrix products, arithmetic and copies ran while one was open for 1% of the time, Pallas kernels for 3%

profile of v7, /device:TPU:8, one launch (start us, length us, event | category | flops | bytes accessed | tf_op | source)
XLA Modules:
  0.0 86.3 jit_solution(6837495210396097078)
XLA Ops:
  0.0 1.8 %shard_map.47 = bf16[512,128]{1,0:T(8,128)(2,1)} custom-call(bf16[3328,512]{1,0:T(8,128)(2,1)} %refs_0_.1, f32[26,512]{1,0:T(8,128)} %refs_1_.1), custom_call_target="tpu_custom_call" | custom-call | flops 53248 | bytes 212992 | tf_op jit(solution)/shard_map/pallas_call | solution.py:55
  1.8 10.4 %all-to-all-start = ((bf16[16,32,128]{2,1,0:T(8,128)(2,1)}), bf16[16,32,128]{2,1,0:T(8,128)(2,1)S(1)}, u32[]{:S(2)}, u32[]{:S(2)}) async-start(bf16[16,32,128]{2,1,0:T(8,128)(2,1)} %bitcast.9), calls=%async_computation | async-start | bytes 262144 | tf_op jit(solution)/shard_map/all_to_all | solution.py:240
  12.2 0.3 multiply_convert_fusion.table_ref
  12.5 1.3 %shard_map.46 = (bf16[128,1664]{1,0:T(8,128)(2,1)S(1)}, bf16[128,1664]{1,0:T(8,128)(2,1)S(1)}, bf16[256,1664]{1,0:T(8,128)(2,1)}) custom-call(bf16[256,3328]{1,0:T(8,128)(2,1)S(1)} %copy-done, s32[1,3328]{1,0:T(1,128)S(1)} %reshape.21.bits_ref, bf16[256,256]{1,0:T(8,128)(2,1)S(1)} %multiply_convert_fusion.table_ref), custom_call_target="tpu_custom_call" | custom-call | flops 436207616 | bytes 3407872 | tf_op jit(solution)/shard_map/pallas_call | solution.py:152
  13.8 3.5 %collective-permute-start = (bf16[256,1664]{1,0:T(8,128)(2,1)}, bf16[256,1664]{1,0:T(8,128)(2,1)S(1)}, u32[]{:S(2)}, u32[]{:S(2)}) collective-permute-start(bf16[256,1664]{1,0:T(8,128)(2,1)} %get-tuple-element.11), channel_id=1, source_target_pairs={{0,128},{128,0},{256,384},{384,256},{1,129},{129,1},{257,385},{385... | collective-permute-start | bytes 2555912 | tf_op jit(solution)/shard_map/ppermute | solution.py:228
  17.3 4.0 %collective-permute-start.3 = (bf16[256,1664]{1,0:T(8,128)(2,1)}, bf16[256,1664]{1,0:T(8,128)(2,1)S(1)}, u32[]{:S(2)}, u32[]{:S(2)}) collective-permute-start(bf16[256,1664]{1,0:T(8,128)(2,1)} %get-tuple-element.11), channel_id=1, source_target_pairs={{0,384},{128,256},{256,128},{384,0},{1,385},{129,257},{257,129},{3... | collective-permute-start | bytes 2555912 | tf_op jit(solution)/shard_map/ppermute | solution.py:228
  21.2 0.0 all-to-all-done
  21.3 0.8 shard_map.48
  22.0 8.7 %all-to-all-start.1 = ((bf16[32,32,128]{2,1,0:T(8,128)(2,1)}), bf16[32,32,128]{2,1,0:T(8,128)(2,1)}, u32[]{:S(2)}, u32[]{:S(2)}) async-start(bf16[32,32,128]{2,1,0:T(8,128)(2,1)} %bitcast.2), calls=%async_computation.1 | async-start | bytes 524288 | tf_op jit(solution)/shard_map/all_to_all | solution.py:250
  30.8 2.6 %collective-permute-start.1 = (bf16[128,1664]{1,0:T(8,128)(2,1)S(1)}, bf16[128,1664]{1,0:T(8,128)(2,1)S(1)}, u32[]{:S(2)}, u32[]{:S(2)}) collective-permute-start(bf16[128,1664]{1,0:T(8,128)(2,1)S(1)} %get-tuple-element.9.refs_0_), channel_id=1, source_target_pairs={{0,256},{128,384},{256,0},{384,128},{1,257},{129,385},{257,1},{385... | collective-permute-start | bytes 1277960 | tf_op jit(solution)/shard_map/ppermute | solution.py:228
  33.4 4.7 %collective-permute-start.2 = (bf16[128,1664]{1,0:T(8,128)(2,1)S(1)}, bf16[128,1664]{1,0:T(8,128)(2,1)S(1)}, u32[]{:S(2)}, u32[]{:S(2)}) collective-permute-start(bf16[128,1664]{1,0:T(8,128)(2,1)S(1)} %get-tuple-element.10.refs_1_), channel_id=1, source_target_pairs={{0,256},{128,384},{256,0},{384,128},{1,257},{129,385},{257,1},{385... | collective-permute-start | bytes 1277960 | tf_op jit(solution)/shard_map/ppermute | solution.py:228
  38.2 3.8 %all-to-all-done.1 = bf16[32,32,128]{2,1,0:T(8,128)(2,1)} async-done(((bf16[32,32,128]{2,1,0:T(8,128)(2,1)}), bf16[32,32,128]{2,1,0:T(8,128)(2,1)}, u32[]{:S(2)}, u32[]{:S(2)}) %all-to-all-start.1) | async-done | bytes 262176 | tf_op jit(solution)/shard_map/all_to_all | solution.py:250
  42.0 0.9 %slice.4 = bf16[2,416,128]{2,1,0:T(8,128)(2,1)S(1)} slice(bf16[2,512,128]{2,1,0:T(8,128)(2,1)} %bitcast.3), slice={[0:2], [0:416], [0:128]} | slice | bytes 425984 | tf_op jit(solution)/shard_map/slice | solution.py:251
  42.9 21.5 %all_gather.3.refs_6_ = bf16[8,416,128]{2,1,0:T(8,128)(2,1)S(1)} all-gather(bf16[2,416,128]{2,1,0:T(8,128)(2,1)S(1)} %slice.4), channel_id=1, replica_groups=mesh['x'=4,'far'=4,'near'=2,'z'=8,'core'=2] {'far'}, dimensions={0}, use_global_device_ids=true | all-gather | bytes 1064960 | tf_op jit(solution)/shard_map/all_gather | solution.py:252
  64.4 0.0 collective-permute-done.1.refs_3_
  64.4 0.0 collective-permute-done.2.refs_4_
  64.4 0.0 collective-permute-done.refs_2_
  64.4 0.8 shard_map.50
  65.3 1.9 %collective-permute-start.4 = (bf16[4,128,256]{2,1,0:T(8,128)(2,1)S(1)}, bf16[4,128,256]{2,1,0:T(8,128)(2,1)S(1)}, u32[]{:S(2)}, u32[]{:S(2)}) collective-permute-start(bf16[4,128,256]{2,1,0:T(8,128)(2,1)S(1)} %shard_map.50), channel_id=1, source_target_pairs={{0,1},{1,0},{2,3},{3,2},{4,5},{5,4},{6,7},{7,6},{8,9},{9,8},{10,11... | collective-permute-start | bytes 786440 | tf_op jit(solution)/shard_map/ppermute | solution.py:256
  67.2 0.8 shard_map.49
  68.0 0.7 collective-permute-done.4
  68.7 0.1 add_convert_fusion
  68.8 16.9 %all_to_all.15 = bf16[32,16,256]{2,1,0:T(8,128)(2,1)S(1)} all-to-all(bf16[32,16,256]{2,1,0:T(8,128)(2,1)S(1)} %bitcast.8), channel_id=1, replica_groups=mesh['x'=4,'far'=4,'near'=2,'z'=8,'core'=2] {'x','z'}, dimensions={0} | all-to-all | bytes 524288 | tf_op jit(solution)/shard_map/all_to_all | solution.py:261
  85.7 0.6 shard_map.51
  (6 shorter events, 0.0 us)
Async XLA Ops:
  0.0 12.2 %copy-start.1 = (s32[3328]{0:T(1024)S(1)}, s32[3328]{0:T(1024)}, u32[]{:S(2)}) copy-start(s32[3328]{0:T(1024)} %param.7) | copy-start | bytes 39940
  0.0 12.5 %copy-start = (bf16[256,3328]{1,0:T(8,128)(2,1)S(1)}, bf16[256,3328]{1,0:T(8,128)(2,1)}, u32[]{:S(2)}) copy-start(bf16[256,3328]{1,0:T(8,128)(2,1)} %hidden_ref.1) | copy-start | bytes 5111812
  1.8 19.5 %all-to-all-start = ((bf16[16,32,128]{2,1,0:T(8,128)(2,1)}), bf16[16,32,128]{2,1,0:T(8,128)(2,1)S(1)}, u32[]{:S(2)}, u32[]{:S(2)}) async-start(bf16[16,32,128]{2,1,0:T(8,128)(2,1)} %bitcast.9), calls=%async_computation | async-start | bytes 262144 | tf_op jit(solution)/shard_map/all_to_all | solution.py:240
  13.8 50.6 %collective-permute-start = (bf16[256,1664]{1,0:T(8,128)(2,1)}, bf16[256,1664]{1,0:T(8,128)(2,1)S(1)}, u32[]{:S(2)}, u32[]{:S(2)}) collective-permute-start(bf16[256,1664]{1,0:T(8,128)(2,1)} %get-tuple-element.11), channel_id=1, source_target_pairs={{0,128},{128,0},{256,384},{384,256},{1,129},{129,1},{257,385},{385... | collective-permute-start | bytes 2555912 | tf_op jit(solution)/shard_map/ppermute | solution.py:228
  17.3 47.2 %collective-permute-start.3 = (bf16[256,1664]{1,0:T(8,128)(2,1)}, bf16[256,1664]{1,0:T(8,128)(2,1)S(1)}, u32[]{:S(2)}, u32[]{:S(2)}) collective-permute-start(bf16[256,1664]{1,0:T(8,128)(2,1)} %get-tuple-element.11), channel_id=1, source_target_pairs={{0,384},{128,256},{256,128},{384,0},{1,385},{129,257},{257,129},{3... | collective-permute-start | bytes 2555912 | tf_op jit(solution)/shard_map/ppermute | solution.py:228
  22.0 20.0 %all-to-all-start.1 = ((bf16[32,32,128]{2,1,0:T(8,128)(2,1)}), bf16[32,32,128]{2,1,0:T(8,128)(2,1)}, u32[]{:S(2)}, u32[]{:S(2)}) async-start(bf16[32,32,128]{2,1,0:T(8,128)(2,1)} %bitcast.2), calls=%async_computation.1 | async-start | bytes 524288 | tf_op jit(solution)/shard_map/all_to_all | solution.py:250
  30.8 33.6 %collective-permute-start.1 = (bf16[128,1664]{1,0:T(8,128)(2,1)S(1)}, bf16[128,1664]{1,0:T(8,128)(2,1)S(1)}, u32[]{:S(2)}, u32[]{:S(2)}) collective-permute-start(bf16[128,1664]{1,0:T(8,128)(2,1)S(1)} %get-tuple-element.9.refs_0_), channel_id=1, source_target_pairs={{0,256},{128,384},{256,0},{384,128},{1,257},{129,385},{257,1},{385... | collective-permute-start | bytes 1277960 | tf_op jit(solution)/shard_map/ppermute | solution.py:228
  33.4 31.0 %collective-permute-start.2 = (bf16[128,1664]{1,0:T(8,128)(2,1)S(1)}, bf16[128,1664]{1,0:T(8,128)(2,1)S(1)}, u32[]{:S(2)}, u32[]{:S(2)}) collective-permute-start(bf16[128,1664]{1,0:T(8,128)(2,1)S(1)} %get-tuple-element.10.refs_1_), channel_id=1, source_target_pairs={{0,256},{128,384},{256,0},{384,128},{1,257},{129,385},{257,1},{385... | collective-permute-start | bytes 1277960 | tf_op jit(solution)/shard_map/ppermute | solution.py:228
  65.3 3.4 %collective-permute-start.4 = (bf16[4,128,256]{2,1,0:T(8,128)(2,1)S(1)}, bf16[4,128,256]{2,1,0:T(8,128)(2,1)S(1)}, u32[]{:S(2)}, u32[]{:S(2)}) collective-permute-start(bf16[4,128,256]{2,1,0:T(8,128)(2,1)S(1)} %shard_map.50), channel_id=1, source_target_pairs={{0,1},{1,0},{2,3},{3,2},{4,5},{5,4},{6,7},{7,6},{8,9},{9,8},{10,11... | collective-permute-start | bytes 786440 | tf_op jit(solution)/shard_map/ppermute | solution.py:256
